TPU v7x, 512 devices: a whole 4x4x16 slice. The times are simulated.
512 devices in a mesh: comp: 2 (over core), gx: 64 (over z, y), gz: 4 (over x).
Axes of the slice: x: 4, y: 4, z: 16, core: 2. Of those that a mesh axis runs over, the one named last changes fastest.
Arguments:
- fields: float32 [2, 72, 1024, 512], P('comp', None, 'gx', 'gz'), may hold values from -6 to 6
- diffusivity: float32 [2, 1024, 512], P('comp', 'gx', 'gz'), may hold values from 0.02 to 0.24
- wet_mask: int32 [1024, 512], P('gx', 'gz'), may hold values 0 or 1
- column_op: float32 [2, 72, 72], P('comp'), as said below
- export_scale: float32 [2, 16], P('comp'), may hold values from 0.5 to 2
- import_gain: float32 [2, 16], P('comp'), may hold values from 0.3 to 1
- tile_source: int32 [2, 1024, 4, 3], P('comp', 'gx', 'gz'), may hold values from 0 to 47
- tile_count: int32 [2, 1024, 4], P('comp', 'gx', 'gz'), may hold values from 1 to 3
- remap_tiles: bfloat16 [2, 1024, 4, 3, 128, 128], P('comp', 'gx', 'gz'), may hold values from -0.3125 to 0.3125
Outputs:
- new_fields: float32 [2, 72, 1024, 512], P('comp', None, 'gx', 'gz')
Inputs may be any that keep to these rules, and one draw needn't show every extreme that they name: A destination tile in grid rows of one device's block reads tile_source in the other component's rows of the block before it along the first grid dimension (values under 16), its own block (16 to 31), or the block after it. `column_op`: each matrix has diagonal entries 0.7.
All inputs are finite; a program needn't handle non-finite values. No bound on the sum of `wet_mask` on one device may be relied on, other than what follows from the above.
Results may differ from a plain program's by a relative error of at most 0.00072.
Values may be sent and summed in bfloat16 or wider, within the bound.
A program may use at most 64 MiB of HBM per device.

v0:
```python
import jax
import jax.numpy as jnp
from jax import lax
from jax.sharding import PartitionSpec as P

MB = 8
FB = 2
NSUB = 4


def partner(block, axis, stride):
    count = lax.axis_size(axis)
    route = []
    for low in range(count):
        high = low | 1 << stride
        if high != low and high < count:
            route += [(low, high), (high, low)]
    return lax.ppermute(block, axis, route)


def extended(cells, sides, width):
    for axis, dim in sides:
        count = lax.axis_size(axis)
        ends = count - 1
        head = lax.slice_in_dim(cells, 0, width, axis=dim)
        tail = lax.slice_in_dim(cells, cells.shape[dim] - width, cells.shape[dim], axis=dim)
        cells = jnp.concatenate(
            [
                lax.ppermute(tail, axis, [(i, (i + 1) % count) for i in range(ends)]),
                cells,
                lax.ppermute(head, axis, [((i + 1) % count, i) for i in range(ends)]),
            ],
            axis=dim,
        )
    return cells


def send_rows(part, rows_dev):
    other = partner(part, "comp", 0)
    return extended(other, (("gx", 1),), rows_dev)


def remap_part(moved, sources, live, tiles):
    picked = moved[:, sources, :] * live[None, :, :, None]
    return jnp.einsum("fxkt,xkts->fxs", picked, tiles, preferred_element_type=jnp.float32)


def couple(exported, sources, live, tiles, rows_dev):
    pieces = [exported[m * FB : (m + 1) * FB] for m in range(MB)]
    results = []
    for piece in pieces:
        moved = send_rows(piece, rows_dev)
        results.append(remap_part(moved, sources, live, tiles))
    return jnp.concatenate(results, axis=0)


def on_device(
    fields,
    diffusivity,
    wet_mask,
    column_op,
    export_scale,
    import_gain,
    tile_source,
    tile_count,
    remap_tiles,
):
    rows_dev = fields.shape[2]
    flux_count = export_scale.shape[1]
    depth = tile_source.shape[3]
    comp_index = lax.axis_index("comp")
    wet = jnp.where(comp_index == 1, wet_mask.astype(jnp.float32), 1.0)
    rate = diffusivity[0] * wet
    sources = tile_source[0, :, 0, :]
    live = (jnp.arange(depth)[None, :] < tile_count[0, :, 0][:, None]).astype(jnp.bfloat16)
    tiles = remap_tiles[0, :, 0]
    operator = column_op[0]
    scales = export_scale[0][:, None, None]
    gains = import_gain[0][:, None, None]
    state = fields[0]
    for step in range(NSUB):
        padded = extended(state, (("gx", 1), ("gz", 2)), 1)
        beside_all = (
            padded[:, 2:, 1:-1] + padded[:, :-2, 1:-1] + padded[:, 1:-1, 2:] + padded[:, 1:-1, :-2]
        )
        smooth = state + rate[None] * (beside_all - 4.0 * state)
        column = jnp.einsum("ab,bxz->axz", operator, smooth, precision=lax.Precision.HIGHEST)
        exported = (jnp.tanh(scales * column[:flux_count]) * wet[None]).astype(jnp.bfloat16)
        imported = couple(exported, sources, live, tiles, rows_dev)
        top = column[:flux_count] + gains * wet[None] * imported
        state = jnp.concatenate([top, column[flux_count:]], axis=0)
    return state[None]


def solution(mesh):
    in_specs = (
        P("comp", None, "gx", "gz"),
        P("comp", "gx", "gz"),
        P("gx", "gz"),
        P("comp", None, None),
        P("comp", None),
        P("comp", None),
        P("comp", "gx", "gz", None),
        P("comp", "gx", "gz"),
        P("comp", "gx", "gz", None, None, None),
    )
    out_specs = P("comp", None, "gx", "gz")
    return jax.shard_map(
        on_device, mesh=mesh, in_specs=in_specs, out_specs=out_specs, check_vma=False
    )
```

profile of v0, /device:TPU:134, one launch (start us, length us, event | category | flops | bytes accessed | tf_op | source)
XLA Modules:
  0.0 516.7 jit_solution(10732345029879452116)
XLA Ops:
  29.2 7.6 %collective-permute-start.27 = (bf16[2,16,128]{2,0,1:T(2,128)(2,1)S(1)}, bf16[2,16,128]{2,0,1:T(2,128)(2,1)S(1)}, u32[]{:S(2)}, u32[]{:S(2)}) collective-permute-start(bf16[2,16,128]{2,0,1:T(2,128)(2,1)S(1)} %collective-permute-done.25), channel_id=1, source_target_pairs={{4,0},{8,4},{12,8},{16,12},{20,16},{24,20},{28,24},{32,28},{36,32}... | collective-permute-start | bytes 24584 | tf_op jit(solution)/shard_map/ppermute | solution.py:31
  45.0 7.2 %collective-permute-start.24 = (bf16[2,16,128]{2,0,1:T(2,128)(2,1)S(1)}, bf16[2,16,128]{2,0,1:T(2,128)(2,1)S(1)}, u32[]{:S(2)}, u32[]{:S(2)}) collective-permute-start(bf16[2,16,128]{2,0,1:T(2,128)(2,1)S(1)} %collective-permute-done.22), channel_id=1, source_target_pairs={{4,0},{8,4},{12,8},{16,12},{20,16},{24,20},{28,24},{32,28},{36,32}... | collective-permute-start | bytes 24584 | tf_op jit(solution)/shard_map/ppermute | solution.py:31
  57.1 7.0 %collective-permute-start.21 = (bf16[2,16,128]{2,0,1:T(2,128)(2,1)S(1)}, bf16[2,16,128]{2,0,1:T(2,128)(2,1)S(1)}, u32[]{:S(2)}, u32[]{:S(2)}) collective-permute-start(bf16[2,16,128]{2,0,1:T(2,128)(2,1)S(1)} %collective-permute-done.19), channel_id=1, source_target_pairs={{4,0},{8,4},{12,8},{16,12},{20,16},{24,20},{28,24},{32,28},{36,32}... | collective-permute-start | bytes 24584 | tf_op jit(solution)/shard_map/ppermute | solution.py:31
  69.8 7.0 %collective-permute-start.18 = (bf16[2,16,128]{2,0,1:T(2,128)(2,1)S(1)}, bf16[2,16,128]{2,0,1:T(2,128)(2,1)S(1)}, u32[]{:S(2)}, u32[]{:S(2)}) collective-permute-start(bf16[2,16,128]{2,0,1:T(2,128)(2,1)S(1)} %collective-permute-done.16), channel_id=1, source_target_pairs={{4,0},{8,4},{12,8},{16,12},{20,16},{24,20},{28,24},{32,28},{36,32}... | collective-permute-start | bytes 24584 | tf_op jit(solution)/shard_map/ppermute | solution.py:31
  91.0 7.2 %collective-permute-start.12 = (bf16[2,16,128]{2,0,1:T(2,128)(2,1)S(1)}, bf16[2,16,128]{2,0,1:T(2,128)(2,1)S(1)}, u32[]{:S(2)}, u32[]{:S(2)}) collective-permute-start(bf16[2,16,128]{2,0,1:T(2,128)(2,1)S(1)} %collective-permute-done.10), channel_id=1, source_target_pairs={{4,0},{8,4},{12,8},{16,12},{20,16},{24,20},{28,24},{32,28},{36,32}... | collective-permute-start | bytes 24584 | tf_op jit(solution)/shard_map/ppermute | solution.py:31
  101.3 7.2 %collective-permute-start.9 = (bf16[2,16,128]{2,0,1:T(2,128)(2,1)S(1)}, bf16[2,16,128]{2,0,1:T(2,128)(2,1)S(1)}, u32[]{:S(2)}, u32[]{:S(2)}) collective-permute-start(bf16[2,16,128]{2,0,1:T(2,128)(2,1)S(1)} %collective-permute-done.7), channel_id=1, source_target_pairs={{4,0},{8,4},{12,8},{16,12},{20,16},{24,20},{28,24},{32,28},{36,32}... | collective-permute-start | bytes 24584 | tf_op jit(solution)/shard_map/ppermute | solution.py:31
  110.5 7.2 %collective-permute-start.6 = (bf16[2,16,128]{2,0,1:T(2,128)(2,1)S(1)}, bf16[2,16,128]{2,0,1:T(2,128)(2,1)S(1)}, u32[]{:S(2)}, u32[]{:S(2)}) collective-permute-start(bf16[2,16,128]{2,0,1:T(2,128)(2,1)S(1)} %collective-permute-done.4), channel_id=1, source_target_pairs={{4,0},{8,4},{12,8},{16,12},{20,16},{24,20},{28,24},{32,28},{36,32}... | collective-permute-start | bytes 24584 | tf_op jit(solution)/shard_map/ppermute | solution.py:31
  131.0 7.2 %collective-permute-start.28 = (f32[72,1,128]{2,0,1:T(8,128)S(1)}, f32[72,1,128]{2,0,1:T(8,128)S(1)}, u32[]{:S(2)}, u32[]{:S(2)}) collective-permute-start(f32[72,1,128]{2,0,1:T(8,128)S(1)} %get-tuple-element.20), channel_id=1, source_target_pairs={{4,0},{8,4},{12,8},{16,12},{20,16},{24,20},{28,24},{32,28},{36,32}... | collective-permute-start | bytes 110600 | tf_op jit(solution)/shard_map/ppermute | solution.py:31
  159.1 7.5 %collective-permute-start.55 = (bf16[2,16,128]{2,0,1:T(2,128)(2,1)S(1)}, bf16[2,16,128]{2,0,1:T(2,128)(2,1)S(1)}, u32[]{:S(2)}, u32[]{:S(2)}) collective-permute-start(bf16[2,16,128]{2,0,1:T(2,128)(2,1)S(1)} %collective-permute-done.53), channel_id=1, source_target_pairs={{4,0},{8,4},{12,8},{16,12},{20,16},{24,20},{28,24},{32,28},{36,32}... | collective-permute-start | bytes 24584 | tf_op jit(solution)/shard_map/ppermute | solution.py:31
  174.9 7.2 %collective-permute-start.52 = (bf16[2,16,128]{2,0,1:T(2,128)(2,1)S(1)}, bf16[2,16,128]{2,0,1:T(2,128)(2,1)S(1)}, u32[]{:S(2)}, u32[]{:S(2)}) collective-permute-start(bf16[2,16,128]{2,0,1:T(2,128)(2,1)S(1)} %collective-permute-done.50), channel_id=1, source_target_pairs={{4,0},{8,4},{12,8},{16,12},{20,16},{24,20},{28,24},{32,28},{36,32}... | collective-permute-start | bytes 24584 | tf_op jit(solution)/shard_map/ppermute | solution.py:31
  187.3 7.0 %collective-permute-start.49 = (bf16[2,16,128]{2,0,1:T(2,128)(2,1)S(1)}, bf16[2,16,128]{2,0,1:T(2,128)(2,1)S(1)}, u32[]{:S(2)}, u32[]{:S(2)}) collective-permute-start(bf16[2,16,128]{2,0,1:T(2,128)(2,1)S(1)} %collective-permute-done.47), channel_id=1, source_target_pairs={{4,0},{8,4},{12,8},{16,12},{20,16},{24,20},{28,24},{32,28},{36,32}... | collective-permute-start | bytes 24584 | tf_op jit(solution)/shard_map/ppermute | solution.py:31
  199.6 7.0 %collective-permute-start.46 = (bf16[2,16,128]{2,0,1:T(2,128)(2,1)S(1)}, bf16[2,16,128]{2,0,1:T(2,128)(2,1)S(1)}, u32[]{:S(2)}, u32[]{:S(2)}) collective-permute-start(bf16[2,16,128]{2,0,1:T(2,128)(2,1)S(1)} %collective-permute-done.44), channel_id=1, source_target_pairs={{4,0},{8,4},{12,8},{16,12},{20,16},{24,20},{28,24},{32,28},{36,32}... | collective-permute-start | bytes 24584 | tf_op jit(solution)/shard_map/ppermute | solution.py:31
  211.8 7.2 %collective-permute-start.43 = (bf16[2,16,128]{2,0,1:T(2,128)(2,1)S(1)}, bf16[2,16,128]{2,0,1:T(2,128)(2,1)S(1)}, u32[]{:S(2)}, u32[]{:S(2)}) collective-permute-start(bf16[2,16,128]{2,0,1:T(2,128)(2,1)S(1)} %collective-permute-done.41), channel_id=1, source_target_pairs={{4,0},{8,4},{12,8},{16,12},{20,16},{24,20},{28,24},{32,28},{36,32}... | collective-permute-start | bytes 24584 | tf_op jit(solution)/shard_map/ppermute | solution.py:31
  221.0 7.2 %collective-permute-start.40 = (bf16[2,16,128]{2,0,1:T(2,128)(2,1)S(1)}, bf16[2,16,128]{2,0,1:T(2,128)(2,1)S(1)}, u32[]{:S(2)}, u32[]{:S(2)}) collective-permute-start(bf16[2,16,128]{2,0,1:T(2,128)(2,1)S(1)} %collective-permute-done.38), channel_id=1, source_target_pairs={{4,0},{8,4},{12,8},{16,12},{20,16},{24,20},{28,24},{32,28},{36,32}... | collective-permute-start | bytes 24584 | tf_op jit(solution)/shard_map/ppermute | solution.py:31
  231.3 7.2 %collective-permute-start.37 = (bf16[2,16,128]{2,0,1:T(2,128)(2,1)S(1)}, bf16[2,16,128]{2,0,1:T(2,128)(2,1)S(1)}, u32[]{:S(2)}, u32[]{:S(2)}) collective-permute-start(bf16[2,16,128]{2,0,1:T(2,128)(2,1)S(1)} %collective-permute-done.35), channel_id=1, source_target_pairs={{4,0},{8,4},{12,8},{16,12},{20,16},{24,20},{28,24},{32,28},{36,32}... | collective-permute-start | bytes 24584 | tf_op jit(solution)/shard_map/ppermute | solution.py:31
  240.5 7.2 %collective-permute-start.34 = (bf16[2,16,128]{2,0,1:T(2,128)(2,1)S(1)}, bf16[2,16,128]{2,0,1:T(2,128)(2,1)S(1)}, u32[]{:S(2)}, u32[]{:S(2)}) collective-permute-start(bf16[2,16,128]{2,0,1:T(2,128)(2,1)S(1)} %collective-permute-done.32), channel_id=1, source_target_pairs={{4,0},{8,4},{12,8},{16,12},{20,16},{24,20},{28,24},{32,28},{36,32}... | collective-permute-start | bytes 24584 | tf_op jit(solution)/shard_map/ppermute | solution.py:31
  261.0 7.2 %collective-permute-start.56 = (f32[72,1,128]{2,0,1:T(8,128)S(1)}, f32[72,1,128]{2,0,1:T(8,128)S(1)}, u32[]{:S(2)}, u32[]{:S(2)}) collective-permute-start(f32[72,1,128]{2,0,1:T(8,128)S(1)} %get-tuple-element.18), channel_id=1, source_target_pairs={{4,0},{8,4},{12,8},{16,12},{20,16},{24,20},{28,24},{32,28},{36,32}... | collective-permute-start | bytes 110600 | tf_op jit(solution)/shard_map/ppermute | solution.py:31
  287.6 7.5 %collective-permute-start.83 = (bf16[2,16,128]{2,0,1:T(2,128)(2,1)S(1)}, bf16[2,16,128]{2,0,1:T(2,128)(2,1)S(1)}, u32[]{:S(2)}, u32[]{:S(2)}) collective-permute-start(bf16[2,16,128]{2,0,1:T(2,128)(2,1)S(1)} %collective-permute-done.81), channel_id=1, source_target_pairs={{4,0},{8,4},{12,8},{16,12},{20,16},{24,20},{28,24},{32,28},{36,32}... | collective-permute-start | bytes 24584 | tf_op jit(solution)/shard_map/ppermute | solution.py:31
  303.4 7.2 %collective-permute-start.80 = (bf16[2,16,128]{2,0,1:T(2,128)(2,1)S(1)}, bf16[2,16,128]{2,0,1:T(2,128)(2,1)S(1)}, u32[]{:S(2)}, u32[]{:S(2)}) collective-permute-start(bf16[2,16,128]{2,0,1:T(2,128)(2,1)S(1)} %collective-permute-done.78), channel_id=1, source_target_pairs={{4,0},{8,4},{12,8},{16,12},{20,16},{24,20},{28,24},{32,28},{36,32}... | collective-permute-start | bytes 24584 | tf_op jit(solution)/shard_map/ppermute | solution.py:31
  328.1 7.0 %collective-permute-start.74 = (bf16[2,16,128]{2,0,1:T(2,128)(2,1)S(1)}, bf16[2,16,128]{2,0,1:T(2,128)(2,1)S(1)}, u32[]{:S(2)}, u32[]{:S(2)}) collective-permute-start(bf16[2,16,128]{2,0,1:T(2,128)(2,1)S(1)} %collective-permute-done.72), channel_id=1, source_target_pairs={{4,0},{8,4},{12,8},{16,12},{20,16},{24,20},{28,24},{32,28},{36,32}... | collective-permute-start | bytes 24584 | tf_op jit(solution)/shard_map/ppermute | solution.py:31
  340.4 7.0 %collective-permute-start.71 = (bf16[2,16,128]{2,0,1:T(2,128)(2,1)S(1)}, bf16[2,16,128]{2,0,1:T(2,128)(2,1)S(1)}, u32[]{:S(2)}, u32[]{:S(2)}) collective-permute-start(bf16[2,16,128]{2,0,1:T(2,128)(2,1)S(1)} %collective-permute-done.69), channel_id=1, source_target_pairs={{4,0},{8,4},{12,8},{16,12},{20,16},{24,20},{28,24},{32,28},{36,32}... | collective-permute-start | bytes 24584 | tf_op jit(solution)/shard_map/ppermute | solution.py:31
  349.4 7.2 %collective-permute-start.68 = (bf16[2,16,128]{2,0,1:T(2,128)(2,1)S(1)}, bf16[2,16,128]{2,0,1:T(2,128)(2,1)S(1)}, u32[]{:S(2)}, u32[]{:S(2)}) collective-permute-start(bf16[2,16,128]{2,0,1:T(2,128)(2,1)S(1)} %collective-permute-done.66), channel_id=1, source_target_pairs={{4,0},{8,4},{12,8},{16,12},{20,16},{24,20},{28,24},{32,28},{36,32}... | collective-permute-start | bytes 24584 | tf_op jit(solution)/shard_map/ppermute | solution.py:31
  359.7 7.2 %collective-permute-start.65 = (bf16[2,16,128]{2,0,1:T(2,128)(2,1)S(1)}, bf16[2,16,128]{2,0,1:T(2,128)(2,1)S(1)}, u32[]{:S(2)}, u32[]{:S(2)}) collective-permute-start(bf16[2,16,128]{2,0,1:T(2,128)(2,1)S(1)} %collective-permute-done.63), channel_id=1, source_target_pairs={{4,0},{8,4},{12,8},{16,12},{20,16},{24,20},{28,24},{32,28},{36,32}... | collective-permute-start | bytes 24584 | tf_op jit(solution)/shard_map/ppermute | solution.py:31
  368.9 7.2 %collective-permute-start.62 = (bf16[2,16,128]{2,0,1:T(2,128)(2,1)S(1)}, bf16[2,16,128]{2,0,1:T(2,128)(2,1)S(1)}, u32[]{:S(2)}, u32[]{:S(2)}) collective-permute-start(bf16[2,16,128]{2,0,1:T(2,128)(2,1)S(1)} %collective-permute-done.60), channel_id=1, source_target_pairs={{4,0},{8,4},{12,8},{16,12},{20,16},{24,20},{28,24},{32,28},{36,32}... | collective-permute-start | bytes 24584 | tf_op jit(solution)/shard_map/ppermute | solution.py:31
  389.4 7.2 %collective-permute-start.84 = (f32[72,1,128]{2,0,1:T(8,128)S(1)}, f32[72,1,128]{2,0,1:T(8,128)S(1)}, u32[]{:S(2)}, u32[]{:S(2)}) collective-permute-start(f32[72,1,128]{2,0,1:T(8,128)S(1)} %get-tuple-element.16), channel_id=1, source_target_pairs={{4,0},{8,4},{12,8},{16,12},{20,16},{24,20},{28,24},{32,28},{36,32}... | collective-permute-start | bytes 110600 | tf_op jit(solution)/shard_map/ppermute | solution.py:31
  415.9 7.6 %collective-permute-start.111 = (bf16[2,16,128]{2,0,1:T(2,128)(2,1)S(1)}, bf16[2,16,128]{2,0,1:T(2,128)(2,1)S(1)}, u32[]{:S(2)}, u32[]{:S(2)}) collective-permute-start(bf16[2,16,128]{2,0,1:T(2,128)(2,1)S(1)} %collective-permute-done.109), channel_id=1, source_target_pairs={{4,0},{8,4},{12,8},{16,12},{20,16},{24,20},{28,24},{32,28},{36,32}... | collective-permute-start | bytes 24584 | tf_op jit(solution)/shard_map/ppermute | solution.py:31
  431.7 7.2 %collective-permute-start.108 = (bf16[2,16,128]{2,0,1:T(2,128)(2,1)S(1)}, bf16[2,16,128]{2,0,1:T(2,128)(2,1)S(1)}, u32[]{:S(2)}, u32[]{:S(2)}) collective-permute-start(bf16[2,16,128]{2,0,1:T(2,128)(2,1)S(1)} %collective-permute-done.106), channel_id=1, source_target_pairs={{4,0},{8,4},{12,8},{16,12},{20,16},{24,20},{28,24},{32,28},{36,32}... | collective-permute-start | bytes 24584 | tf_op jit(solution)/shard_map/ppermute | solution.py:31
  444.2 7.0 %collective-permute-start.105 = (bf16[2,16,128]{2,0,1:T(2,128)(2,1)S(1)}, bf16[2,16,128]{2,0,1:T(2,128)(2,1)S(1)}, u32[]{:S(2)}, u32[]{:S(2)}) collective-permute-start(bf16[2,16,128]{2,0,1:T(2,128)(2,1)S(1)} %collective-permute-done.103), channel_id=1, source_target_pairs={{4,0},{8,4},{12,8},{16,12},{20,16},{24,20},{28,24},{32,28},{36,32}... | collective-permute-start | bytes 24584 | tf_op jit(solution)/shard_map/ppermute | solution.py:31
  456.4 7.0 %collective-permute-start.102 = (bf16[2,16,128]{2,0,1:T(2,128)(2,1)S(1)}, bf16[2,16,128]{2,0,1:T(2,128)(2,1)S(1)}, u32[]{:S(2)}, u32[]{:S(2)}) collective-permute-start(bf16[2,16,128]{2,0,1:T(2,128)(2,1)S(1)} %collective-permute-done.100), channel_id=1, source_target_pairs={{4,0},{8,4},{12,8},{16,12},{20,16},{24,20},{28,24},{32,28},{36,32}... | collective-permute-start | bytes 24584 | tf_op jit(solution)/shard_map/ppermute | solution.py:31
  477.6 7.2 %collective-permute-start.96 = (bf16[2,16,128]{2,0,1:T(2,128)(2,1)S(1)}, bf16[2,16,128]{2,0,1:T(2,128)(2,1)S(1)}, u32[]{:S(2)}, u32[]{:S(2)}) collective-permute-start(bf16[2,16,128]{2,0,1:T(2,128)(2,1)S(1)} %collective-permute-done.94), channel_id=1, source_target_pairs={{4,0},{8,4},{12,8},{16,12},{20,16},{24,20},{28,24},{32,28},{36,32}... | collective-permute-start | bytes 24584 | tf_op jit(solution)/shard_map/ppermute | solution.py:31
  488.0 7.2 %collective-permute-start.93 = (bf16[2,16,128]{2,0,1:T(2,128)(2,1)S(1)}, bf16[2,16,128]{2,0,1:T(2,128)(2,1)S(1)}, u32[]{:S(2)}, u32[]{:S(2)}) collective-permute-start(bf16[2,16,128]{2,0,1:T(2,128)(2,1)S(1)} %collective-permute-done.91), channel_id=1, source_target_pairs={{4,0},{8,4},{12,8},{16,12},{20,16},{24,20},{28,24},{32,28},{36,32}... | collective-permute-start | bytes 24584 | tf_op jit(solution)/shard_map/ppermute | solution.py:31
  497.2 7.2 %collective-permute-start.90 = (bf16[2,16,128]{2,0,1:T(2,128)(2,1)S(1)}, bf16[2,16,128]{2,0,1:T(2,128)(2,1)S(1)}, u32[]{:S(2)}, u32[]{:S(2)}) collective-permute-start(bf16[2,16,128]{2,0,1:T(2,128)(2,1)S(1)} %collective-permute-done.88), channel_id=1, source_target_pairs={{4,0},{8,4},{12,8},{16,12},{20,16},{24,20},{28,24},{32,28},{36,32}... | collective-permute-start | bytes 24584 | tf_op jit(solution)/shard_map/ppermute | solution.py:31
  (389 shorter events, 283.2 us)
Async XLA Ops:
  40.7 26.9 %collective-permute-start.16 = (bf16[2,16,128]{2,0,1:T(2,128)(2,1)S(1)}, bf16[2,16,128]{2,0,1:T(2,128)(2,1)S(1)}, u32[]{:S(2)}, u32[]{:S(2)}) collective-permute-start(bf16[2,16,128]{2,0,1:T(2,128)(2,1)S(1)} %get-tuple-element.50), channel_id=1, source_target_pairs={{0,256},{256,0},{1,257},{257,1},{2,258},{258,2},{3,259},{259,3},{4... | collective-permute-start | bytes 24584 | tf_op jit(solution)/shard_map/ppermute | solution.py:18
  43.1 36.8 %collective-permute-start.13 = (bf16[2,16,128]{2,0,1:T(2,128)(2,1)S(1)}, bf16[2,16,128]{2,0,1:T(2,128)(2,1)S(1)}, u32[]{:S(2)}, u32[]{:S(2)}) collective-permute-start(bf16[2,16,128]{2,0,1:T(2,128)(2,1)S(1)} %get-tuple-element.51), channel_id=1, source_target_pairs={{0,256},{256,0},{1,257},{257,1},{2,258},{258,2},{3,259},{259,3},{4... | collective-permute-start | bytes 24584 | tf_op jit(solution)/shard_map/ppermute | solution.py:18
  54.9 27.1 %collective-permute-start.10 = (bf16[2,16,128]{2,0,1:T(2,128)(2,1)S(1)}, bf16[2,16,128]{2,0,1:T(2,128)(2,1)S(1)}, u32[]{:S(2)}, u32[]{:S(2)}) collective-permute-start(bf16[2,16,128]{2,0,1:T(2,128)(2,1)S(1)} %get-tuple-element.52), channel_id=1, source_target_pairs={{0,256},{256,0},{1,257},{257,1},{2,258},{258,2},{3,259},{259,3},{4... | collective-permute-start | bytes 24584 | tf_op jit(solution)/shard_map/ppermute | solution.py:18
  67.6 31.8 %collective-permute-start.7 = (bf16[2,16,128]{2,0,1:T(2,128)(2,1)S(1)}, bf16[2,16,128]{2,0,1:T(2,128)(2,1)S(1)}, u32[]{:S(2)}, u32[]{:S(2)}) collective-permute-start(bf16[2,16,128]{2,0,1:T(2,128)(2,1)S(1)} %get-tuple-element.53), channel_id=1, source_target_pairs={{0,256},{256,0},{1,257},{257,1},{2,258},{258,2},{3,259},{259,3},{4... | collective-permute-start | bytes 24584 | tf_op jit(solution)/shard_map/ppermute | solution.py:18
  79.9 21.4 %collective-permute-start.4 = (bf16[2,16,128]{2,0,1:T(2,128)(2,1)S(1)}, bf16[2,16,128]{2,0,1:T(2,128)(2,1)S(1)}, u32[]{:S(2)}, u32[]{:S(2)}) collective-permute-start(bf16[2,16,128]{2,0,1:T(2,128)(2,1)S(1)} %get-tuple-element.54), channel_id=1, source_target_pairs={{0,256},{256,0},{1,257},{257,1},{2,258},{258,2},{3,259},{259,3},{4... | collective-permute-start | bytes 24584 | tf_op jit(solution)/shard_map/ppermute | solution.py:18
  82.0 26.6 %collective-permute-start.15 = (bf16[2,16,128]{2,0,1:T(2,128)(2,1)S(1)}, bf16[2,16,128]{2,0,1:T(2,128)(2,1)S(1)}, u32[]{:S(2)}, u32[]{:S(2)}) collective-permute-start(bf16[2,16,128]{2,0,1:T(2,128)(2,1)S(1)} %collective-permute-done.13), channel_id=1, source_target_pairs={{4,0},{8,4},{12,8},{16,12},{20,16},{24,20},{28,24},{32,28},{36,32}... | collective-permute-start | bytes 24584 | tf_op jit(solution)/shard_map/ppermute | solution.py:31
  91.0 27.9 %collective-permute-start.12 = (bf16[2,16,128]{2,0,1:T(2,128)(2,1)S(1)}, bf16[2,16,128]{2,0,1:T(2,128)(2,1)S(1)}, u32[]{:S(2)}, u32[]{:S(2)}) collective-permute-start(bf16[2,16,128]{2,0,1:T(2,128)(2,1)S(1)} %collective-permute-done.10), channel_id=1, source_target_pairs={{4,0},{8,4},{12,8},{16,12},{20,16},{24,20},{28,24},{32,28},{36,32}... | collective-permute-start | bytes 24584 | tf_op jit(solution)/shard_map/ppermute | solution.py:31
  99.4 21.4 %collective-permute-start.11 = (bf16[2,16,128]{2,0,1:T(2,128)(2,1)S(1)}, bf16[2,16,128]{2,0,1:T(2,128)(2,1)S(1)}, u32[]{:S(2)}, u32[]{:S(2)}) collective-permute-start(bf16[2,16,128]{2,0,1:T(2,128)(2,1)S(1)} %collective-permute-done.10), channel_id=1, source_target_pairs={{0,4},{4,8},{8,12},{12,16},{16,20},{20,24},{24,28},{28,32},{32,36}... | collective-permute-start | bytes 24584 | tf_op jit(solution)/shard_map/ppermute | solution.py:29
  170.5 26.9 %collective-permute-start.44 = (bf16[2,16,128]{2,0,1:T(2,128)(2,1)S(1)}, bf16[2,16,128]{2,0,1:T(2,128)(2,1)S(1)}, u32[]{:S(2)}, u32[]{:S(2)}) collective-permute-start(bf16[2,16,128]{2,0,1:T(2,128)(2,1)S(1)} %get-tuple-element.42), channel_id=1, source_target_pairs={{0,256},{256,0},{1,257},{257,1},{2,258},{258,2},{3,259},{259,3},{4... | collective-permute-start | bytes 24584 | tf_op jit(solution)/shard_map/ppermute | solution.py:18
  172.9 36.7 %collective-permute-start.41 = (bf16[2,16,128]{2,0,1:T(2,128)(2,1)S(1)}, bf16[2,16,128]{2,0,1:T(2,128)(2,1)S(1)}, u32[]{:S(2)}, u32[]{:S(2)}) collective-permute-start(bf16[2,16,128]{2,0,1:T(2,128)(2,1)S(1)} %get-tuple-element.43), channel_id=1, source_target_pairs={{0,256},{256,0},{1,257},{257,1},{2,258},{258,2},{3,259},{259,3},{4... | collective-permute-start | bytes 24584 | tf_op jit(solution)/shard_map/ppermute | solution.py:18
  185.2 26.6 %collective-permute-start.38 = (bf16[2,16,128]{2,0,1:T(2,128)(2,1)S(1)}, bf16[2,16,128]{2,0,1:T(2,128)(2,1)S(1)}, u32[]{:S(2)}, u32[]{:S(2)}) collective-permute-start(bf16[2,16,128]{2,0,1:T(2,128)(2,1)S(1)} %get-tuple-element.44), channel_id=1, source_target_pairs={{0,256},{256,0},{1,257},{257,1},{2,258},{258,2},{3,259},{259,3},{4... | collective-permute-start | bytes 24584 | tf_op jit(solution)/shard_map/ppermute | solution.py:18
  197.4 31.9 %collective-permute-start.35 = (bf16[2,16,128]{2,0,1:T(2,128)(2,1)S(1)}, bf16[2,16,128]{2,0,1:T(2,128)(2,1)S(1)}, u32[]{:S(2)}, u32[]{:S(2)}) collective-permute-start(bf16[2,16,128]{2,0,1:T(2,128)(2,1)S(1)} %get-tuple-element.45), channel_id=1, source_target_pairs={{0,256},{256,0},{1,257},{257,1},{2,258},{258,2},{3,259},{259,3},{4... | collective-permute-start | bytes 24584 | tf_op jit(solution)/shard_map/ppermute | solution.py:18
  209.7 21.6 %collective-permute-start.32 = (bf16[2,16,128]{2,0,1:T(2,128)(2,1)S(1)}, bf16[2,16,128]{2,0,1:T(2,128)(2,1)S(1)}, u32[]{:S(2)}, u32[]{:S(2)}) collective-permute-start(bf16[2,16,128]{2,0,1:T(2,128)(2,1)S(1)} %get-tuple-element.46), channel_id=1, source_target_pairs={{0,256},{256,0},{1,257},{257,1},{2,258},{258,2},{3,259},{259,3},{4... | collective-permute-start | bytes 24584 | tf_op jit(solution)/shard_map/ppermute | solution.py:18
  211.8 26.7 %collective-permute-start.43 = (bf16[2,16,128]{2,0,1:T(2,128)(2,1)S(1)}, bf16[2,16,128]{2,0,1:T(2,128)(2,1)S(1)}, u32[]{:S(2)}, u32[]{:S(2)}) collective-permute-start(bf16[2,16,128]{2,0,1:T(2,128)(2,1)S(1)} %collective-permute-done.41), channel_id=1, source_target_pairs={{4,0},{8,4},{12,8},{16,12},{20,16},{24,20},{28,24},{32,28},{36,32}... | collective-permute-start | bytes 24584 | tf_op jit(solution)/shard_map/ppermute | solution.py:31
  221.0 27.9 %collective-permute-start.40 = (bf16[2,16,128]{2,0,1:T(2,128)(2,1)S(1)}, bf16[2,16,128]{2,0,1:T(2,128)(2,1)S(1)}, u32[]{:S(2)}, u32[]{:S(2)}) collective-permute-start(bf16[2,16,128]{2,0,1:T(2,128)(2,1)S(1)} %collective-permute-done.38), channel_id=1, source_target_pairs={{4,0},{8,4},{12,8},{16,12},{20,16},{24,20},{28,24},{32,28},{36,32}... | collective-permute-start | bytes 24584 | tf_op jit(solution)/shard_map/ppermute | solution.py:31
  229.4 21.4 %collective-permute-start.39 = (bf16[2,16,128]{2,0,1:T(2,128)(2,1)S(1)}, bf16[2,16,128]{2,0,1:T(2,128)(2,1)S(1)}, u32[]{:S(2)}, u32[]{:S(2)}) collective-permute-start(bf16[2,16,128]{2,0,1:T(2,128)(2,1)S(1)} %collective-permute-done.38), channel_id=1, source_target_pairs={{0,4},{4,8},{8,12},{12,16},{16,20},{20,24},{24,28},{28,32},{32,36}... | collective-permute-start | bytes 24584 | tf_op jit(solution)/shard_map/ppermute | solution.py:29
  299.1 26.9 %collective-permute-start.72 = (bf16[2,16,128]{2,0,1:T(2,128)(2,1)S(1)}, bf16[2,16,128]{2,0,1:T(2,128)(2,1)S(1)}, u32[]{:S(2)}, u32[]{:S(2)}) collective-permute-start(bf16[2,16,128]{2,0,1:T(2,128)(2,1)S(1)} %get-tuple-element.34), channel_id=1, source_target_pairs={{0,256},{256,0},{1,257},{257,1},{2,258},{258,2},{3,259},{259,3},{4... | collective-permute-start | bytes 24584 | tf_op jit(solution)/shard_map/ppermute | solution.py:18
  301.5 36.7 %collective-permute-start.69 = (bf16[2,16,128]{2,0,1:T(2,128)(2,1)S(1)}, bf16[2,16,128]{2,0,1:T(2,128)(2,1)S(1)}, u32[]{:S(2)}, u32[]{:S(2)}) collective-permute-start(bf16[2,16,128]{2,0,1:T(2,128)(2,1)S(1)} %get-tuple-element.35), channel_id=1, source_target_pairs={{0,256},{256,0},{1,257},{257,1},{2,258},{258,2},{3,259},{259,3},{4... | collective-permute-start | bytes 24584 | tf_op jit(solution)/shard_map/ppermute | solution.py:18
  313.7 26.6 %collective-permute-start.66 = (bf16[2,16,128]{2,0,1:T(2,128)(2,1)S(1)}, bf16[2,16,128]{2,0,1:T(2,128)(2,1)S(1)}, u32[]{:S(2)}, u32[]{:S(2)}) collective-permute-start(bf16[2,16,128]{2,0,1:T(2,128)(2,1)S(1)} %get-tuple-element.36), channel_id=1, source_target_pairs={{0,256},{256,0},{1,257},{257,1},{2,258},{258,2},{3,259},{259,3},{4... | collective-permute-start | bytes 24584 | tf_op jit(solution)/shard_map/ppermute | solution.py:18
  326.0 31.8 %collective-permute-start.63 = (bf16[2,16,128]{2,0,1:T(2,128)(2,1)S(1)}, bf16[2,16,128]{2,0,1:T(2,128)(2,1)S(1)}, u32[]{:S(2)}, u32[]{:S(2)}) collective-permute-start(bf16[2,16,128]{2,0,1:T(2,128)(2,1)S(1)} %get-tuple-element.37), channel_id=1, source_target_pairs={{0,256},{256,0},{1,257},{257,1},{2,258},{258,2},{3,259},{259,3},{4... | collective-permute-start | bytes 24584 | tf_op jit(solution)/shard_map/ppermute | solution.py:18
  338.2 21.4 %collective-permute-start.60 = (bf16[2,16,128]{2,0,1:T(2,128)(2,1)S(1)}, bf16[2,16,128]{2,0,1:T(2,128)(2,1)S(1)}, u32[]{:S(2)}, u32[]{:S(2)}) collective-permute-start(bf16[2,16,128]{2,0,1:T(2,128)(2,1)S(1)} %get-tuple-element.38), channel_id=1, source_target_pairs={{0,256},{256,0},{1,257},{257,1},{2,258},{258,2},{3,259},{259,3},{4... | collective-permute-start | bytes 24584 | tf_op jit(solution)/shard_map/ppermute | solution.py:18
  340.4 26.6 %collective-permute-start.71 = (bf16[2,16,128]{2,0,1:T(2,128)(2,1)S(1)}, bf16[2,16,128]{2,0,1:T(2,128)(2,1)S(1)}, u32[]{:S(2)}, u32[]{:S(2)}) collective-permute-start(bf16[2,16,128]{2,0,1:T(2,128)(2,1)S(1)} %collective-permute-done.69), channel_id=1, source_target_pairs={{4,0},{8,4},{12,8},{16,12},{20,16},{24,20},{28,24},{32,28},{36,32}... | collective-permute-start | bytes 24584 | tf_op jit(solution)/shard_map/ppermute | solution.py:31
  349.4 27.9 %collective-permute-start.68 = (bf16[2,16,128]{2,0,1:T(2,128)(2,1)S(1)}, bf16[2,16,128]{2,0,1:T(2,128)(2,1)S(1)}, u32[]{:S(2)}, u32[]{:S(2)}) collective-permute-start(bf16[2,16,128]{2,0,1:T(2,128)(2,1)S(1)} %collective-permute-done.66), channel_id=1, source_target_pairs={{4,0},{8,4},{12,8},{16,12},{20,16},{24,20},{28,24},{32,28},{36,32}... | collective-permute-start | bytes 24584 | tf_op jit(solution)/shard_map/ppermute | solution.py:31
  357.7 21.4 %collective-permute-start.67 = (bf16[2,16,128]{2,0,1:T(2,128)(2,1)S(1)}, bf16[2,16,128]{2,0,1:T(2,128)(2,1)S(1)}, u32[]{:S(2)}, u32[]{:S(2)}) collective-permute-start(bf16[2,16,128]{2,0,1:T(2,128)(2,1)S(1)} %collective-permute-done.66), channel_id=1, source_target_pairs={{0,4},{4,8},{8,12},{12,16},{16,20},{20,24},{24,28},{28,32},{32,36}... | collective-permute-start | bytes 24584 | tf_op jit(solution)/shard_map/ppermute | solution.py:29
  427.3 26.9 %collective-permute-start.100 = (bf16[2,16,128]{2,0,1:T(2,128)(2,1)S(1)}, bf16[2,16,128]{2,0,1:T(2,128)(2,1)S(1)}, u32[]{:S(2)}, u32[]{:S(2)}) collective-permute-start(bf16[2,16,128]{2,0,1:T(2,128)(2,1)S(1)} %get-tuple-element.26), channel_id=1, source_target_pairs={{0,256},{256,0},{1,257},{257,1},{2,258},{258,2},{3,259},{259,3},{4... | collective-permute-start | bytes 24584 | tf_op jit(solution)/shard_map/ppermute | solution.py:18
  429.8 36.7 %collective-permute-start.97 = (bf16[2,16,128]{2,0,1:T(2,128)(2,1)S(1)}, bf16[2,16,128]{2,0,1:T(2,128)(2,1)S(1)}, u32[]{:S(2)}, u32[]{:S(2)}) collective-permute-start(bf16[2,16,128]{2,0,1:T(2,128)(2,1)S(1)} %get-tuple-element.27), channel_id=1, source_target_pairs={{0,256},{256,0},{1,257},{257,1},{2,258},{258,2},{3,259},{259,3},{4... | collective-permute-start | bytes 24584 | tf_op jit(solution)/shard_map/ppermute | solution.py:18
  442.0 26.6 %collective-permute-start.94 = (bf16[2,16,128]{2,0,1:T(2,128)(2,1)S(1)}, bf16[2,16,128]{2,0,1:T(2,128)(2,1)S(1)}, u32[]{:S(2)}, u32[]{:S(2)}) collective-permute-start(bf16[2,16,128]{2,0,1:T(2,128)(2,1)S(1)} %get-tuple-element.28), channel_id=1, source_target_pairs={{0,256},{256,0},{1,257},{257,1},{2,258},{258,2},{3,259},{259,3},{4... | collective-permute-start | bytes 24584 | tf_op jit(solution)/shard_map/ppermute | solution.py:18
  454.3 31.8 %collective-permute-start.91 = (bf16[2,16,128]{2,0,1:T(2,128)(2,1)S(1)}, bf16[2,16,128]{2,0,1:T(2,128)(2,1)S(1)}, u32[]{:S(2)}, u32[]{:S(2)}) collective-permute-start(bf16[2,16,128]{2,0,1:T(2,128)(2,1)S(1)} %get-tuple-element.29), channel_id=1, source_target_pairs={{0,256},{256,0},{1,257},{257,1},{2,258},{258,2},{3,259},{259,3},{4... | collective-permute-start | bytes 24584 | tf_op jit(solution)/shard_map/ppermute | solution.py:18
  466.5 21.4 %collective-permute-start.88 = (bf16[2,16,128]{2,0,1:T(2,128)(2,1)S(1)}, bf16[2,16,128]{2,0,1:T(2,128)(2,1)S(1)}, u32[]{:S(2)}, u32[]{:S(2)}) collective-permute-start(bf16[2,16,128]{2,0,1:T(2,128)(2,1)S(1)} %get-tuple-element.30), channel_id=1, source_target_pairs={{0,256},{256,0},{1,257},{257,1},{2,258},{258,2},{3,259},{259,3},{4... | collective-permute-start | bytes 24584 | tf_op jit(solution)/shard_map/ppermute | solution.py:18
  468.7 26.6 %collective-permute-start.99 = (bf16[2,16,128]{2,0,1:T(2,128)(2,1)S(1)}, bf16[2,16,128]{2,0,1:T(2,128)(2,1)S(1)}, u32[]{:S(2)}, u32[]{:S(2)}) collective-permute-start(bf16[2,16,128]{2,0,1:T(2,128)(2,1)S(1)} %collective-permute-done.97), channel_id=1, source_target_pairs={{4,0},{8,4},{12,8},{16,12},{20,16},{24,20},{28,24},{32,28},{36,32}... | collective-permute-start | bytes 24584 | tf_op jit(solution)/shard_map/ppermute | solution.py:31
  477.6 27.9 %collective-permute-start.96 = (bf16[2,16,128]{2,0,1:T(2,128)(2,1)S(1)}, bf16[2,16,128]{2,0,1:T(2,128)(2,1)S(1)}, u32[]{:S(2)}, u32[]{:S(2)}) collective-permute-start(bf16[2,16,128]{2,0,1:T(2,128)(2,1)S(1)} %collective-permute-done.94), channel_id=1, source_target_pairs={{4,0},{8,4},{12,8},{16,12},{20,16},{24,20},{28,24},{32,28},{36,32}... | collective-permute-start | bytes 24584 | tf_op jit(solution)/shard_map/ppermute | solution.py:31
  486.0 21.4 %collective-permute-start.95 = (bf16[2,16,128]{2,0,1:T(2,128)(2,1)S(1)}, bf16[2,16,128]{2,0,1:T(2,128)(2,1)S(1)}, u32[]{:S(2)}, u32[]{:S(2)}) collective-permute-start(bf16[2,16,128]{2,0,1:T(2,128)(2,1)S(1)} %collective-permute-done.94), channel_id=1, source_target_pairs={{0,4},{4,8},{8,12},{12,16},{16,20},{20,24},{24,28},{28,32},{32,36}... | collective-permute-start | bytes 24584 | tf_op jit(solution)/shard_map/ppermute | solution.py:29
  (100 other events, 1383.2 us)
where the time goes:
time: 520 us; the launch traced here: 517 us
  starting transfers between devices  416 us (80%)
  waiting for transfers between devices  37.2 us (7%)
  local copies, waits for them, and re-layouts  34.2 us (7%)
  matrix products  22.9 us (4%)
    ppermute x40, starting transfers between devices, extended(): lax.ppermute(head, axis, [((i + 1) % count, i) for i in range(ends)])  272 us
    ppermute x40, starting transfers between devices, extended(): lax.ppermute(tail, axis, [(i, (i + 1) % count) for i in range(ends)])  76 us
    ppermute x32, starting transfers between devices, partner(): return lax.ppermute(block, axis, route)  68.1 us
    ppermute x40, waiting for transfers between devices, extended(): lax.ppermute(tail, axis, [(i, (i + 1) % count) for i in range(ends)])  30.7 us
    gather x32, local copies, waits for them, and re-layouts, remap_part(): picked = moved[:, sources, :] * live[None, :, :, None]  19.9 us
    dot_general x32, matrix products, remap_part(): jnp.einsum('fxkt,xkts->fxs', picked, tiles, preferred_element_type=jnp.fl...  14.1 us
  transfers between devices with their start and end apart: 112, of which 12 were waited for; matrix products, arithmetic and copies ran while one was open for 7% of the time, Pallas kernels for 0%

commit v1 on v0

v1 whole, which is shorter than its diff:
```python
import functools

import jax
import jax.numpy as jnp
from jax import lax
from jax.experimental import pallas as pl
from jax.experimental.pallas import tpu as pltpu
from jax.sharding import PartitionSpec as P

NSUB = 4
MESH = pl.DeviceIdType.MESH
F32 = jnp.float32
BF16 = jnp.bfloat16


def lane_ids(shape):
    return lax.broadcasted_iota(jnp.int32, shape, 1)


def split3(value, pad):
    if pad:
        value = jnp.concatenate([value, jnp.zeros((pad, value.shape[1]), F32)], axis=0)
    high = value.astype(BF16)
    low = (value - high.astype(F32)).astype(BF16)
    return [high, high, low]


def kernel(
    dims,
    fields,
    diff,
    wetm,
    op,
    scale,
    gain,
    source,
    count,
    tiles,
    out,
    pad,
    dpad,
    hz,
    dz,
    ex0,
    ex1,
    ex2,
    ex3,
    es,
    ppre,
    last,
    zpack,
    dzpack,
    w,
    rate,
    weti,
    wet,
    ops,
    acat,
    acat16,
    state_sem,
    misc_sem,
    out_sem,
    hx_send,
    hx_recv,
    hz_send,
    hz_recv,
    dx_send,
    dx_recv,
    dz_send,
    dz_recv,
    ex_send,
    ex_recv,
):
    lev, rows, flux, depth = dims
    exs = (ex0, ex1, ex2, ex3)
    groups = lev // 8
    fgroups = flux // 8
    c, gx, gz = lax.axis_index("comp"), lax.axis_index("gx"), lax.axis_index("gz")
    nx, nz = lax.axis_size("gx"), lax.axis_size("gz")
    prev, nxt, left, right = gx > 0, gx < nx - 1, gz > 0, gz < nz - 1
    at_prev, at_next = (c, gx - 1, gz), (c, gx + 1, gz)
    at_left, at_right = (c, gx, gz - 1), (c, gx, gz + 1)
    over = (1 - c, gx, gz)
    over_prev, over_next = (1 - c, gx - 1, gz), (1 - c, gx + 1, gz)

    state_copies = [
        pltpu.make_async_copy(
            fields.at[0, :, r, :], pad.at[0, r + 1], state_sem.at[r]
        )
        for r in range(rows)
    ]
    misc = [
        pltpu.make_async_copy(diff.at[0], rate, misc_sem.at[0]),
        pltpu.make_async_copy(wetm, weti, misc_sem.at[1]),
        pltpu.make_async_copy(op.at[0], ops, misc_sem.at[2]),
    ]
    tile_copy = pltpu.make_async_copy(tiles.at[0, :, 0], w, misc_sem.at[3])
    for copy in state_copies + misc + [tile_copy]:
        copy.start()

    @pl.when(jnp.logical_not(prev))
    def _():
        pad[:, 0] = jnp.zeros((NSUB, lev, 128), F32)
        dpad[:, 0] = jnp.zeros((NSUB - 1, flux, 128), F32)
        for ref in exs:
            ref[0:rows] = jnp.zeros((rows, flux, 128), BF16)

    @pl.when(jnp.logical_not(nxt))
    def _():
        pad[:, rows + 1] = jnp.zeros((NSUB, lev, 128), F32)
        dpad[:, rows + 1] = jnp.zeros((NSUB - 1, flux, 128), F32)
        for ref in exs:
            ref[2 * rows : 3 * rows] = jnp.zeros((rows, flux, 128), BF16)

    @pl.when(jnp.logical_not(left))
    def _():
        hz[:, 0] = jnp.zeros((NSUB, 16, 128), F32)
        dz[:, 0] = jnp.zeros((NSUB - 1, 8, 128), F32)

    @pl.when(jnp.logical_not(right))
    def _():
        hz[:, 1] = jnp.zeros((NSUB, 16, 128), F32)
        dz[:, 1] = jnp.zeros((NSUB - 1, 8, 128), F32)

    for ref in exs:
        ref[3 * rows] = jnp.zeros((flux, 128), BF16)

    barrier = pltpu.get_barrier_semaphore()
    peers = [
        (None, over),
        (prev, over_prev),
        (prev, at_prev),
        (nxt, over_next),
        (nxt, at_next),
        (left, at_left),
        (right, at_right),
    ]

    def when(flag, body):
        if flag is None:
            body()
        else:
            pl.when(flag)(body)

    for flag, peer in peers:
        when(
            flag,
            lambda peer=peer: pl.semaphore_signal(
                barrier, inc=1, device_id=peer, device_id_type=MESH
            ),
        )
    expected = (
        1
        + 2 * prev.astype(jnp.int32)
        + 2 * nxt.astype(jnp.int32)
        + left.astype(jnp.int32)
        + right.astype(jnp.int32)
    )
    pl.semaphore_wait(barrier, expected)

    sent = []

    def remote(flag, src, dst, ssem, rsem, peer, start=True):
        copy = pltpu.make_async_remote_copy(
            src_ref=src,
            dst_ref=dst,
            send_sem=ssem,
            recv_sem=rsem,
            device_id=peer,
            device_id_type=MESH,
        )
        if start:
            when(flag, copy.start)
            sent.append((flag, copy))
        return copy

    def receive(flag, dst, rsem, peer):
        copy = pltpu.make_async_remote_copy(
            src_ref=dst,
            dst_ref=dst,
            send_sem=rsem,
            recv_sem=rsem,
            device_id=peer,
            device_id_type=MESH,
        )
        when(flag, copy.wait_recv)

    def send_rows(first, last_row, box, t, send, recv):
        remote(prev, first, box.at[t, rows + 1], send.at[t, 1], recv.at[t, 1], at_prev)
        remote(nxt, last_row, box.at[t, 0], send.at[t, 0], recv.at[t, 0], at_next)

    def wait_rows(box, t, recv):
        receive(prev, box.at[t, 0], recv.at[t, 0], at_prev)
        receive(nxt, box.at[t, rows + 1], recv.at[t, 1], at_next)

    def send_columns(pack, box, t, send, recv):
        remote(left, pack.at[t, 1], box.at[t, 1], send.at[t, 1], recv.at[t, 1], at_left)
        remote(right, pack.at[t, 0], box.at[t, 0], send.at[t, 0], recv.at[t, 0], at_right)

    def wait_columns(box, t, recv):
        receive(left, box.at[t, 0], recv.at[t, 0], at_left)
        receive(right, box.at[t, 1], recv.at[t, 1], at_right)

    lane8 = lane_ids((8, 128))

    def pack_edges(load, n_groups):
        parts = [[None, None], [None, None]]
        for r in range(rows):
            for g in range(n_groups):
                value = load(r, g)
                half, lane = divmod(g * rows + r, 128)
                for side, have in ((0, 127), (1, 0)):
                    moved = pltpu.roll(value, (lane - have) % 128, 1) if lane != have else value
                    old = parts[side][half]
                    parts[side][half] = (
                        moved if old is None else jnp.where(lane8 == lane, moved, old)
                    )
        return parts

    def stencil(load, packed, n_groups, r):
        here = load(r + 1)
        levels = 8 * n_groups
        lane = lane_ids((levels, 128))
        lefts, rights = [], []
        for g in range(n_groups):
            half, at = divmod(g * rows + r, 128)
            lefts.append(pltpu.roll(packed[0][half], (0 - at) % 128, 1) if at != 0 else packed[0][half])
            rights.append(
                pltpu.roll(packed[1][half], (127 - at) % 128, 1) if at != 127 else packed[1][half]
            )
        before = jnp.where(lane == 0, jnp.concatenate(lefts, axis=0), pltpu.roll(here, 1, 1))
        after = jnp.where(lane == 127, jnp.concatenate(rights, axis=0), pltpu.roll(here, 127, 1))
        beside = load(r + 2) + load(r) + after + before
        return here + rate[r : r + 1, :] * (beside - 4.0 * here)

    send_rows(fields.at[0, :, 0, :], fields.at[0, :, rows - 1, :], pad, 0, hx_send, hx_recv)

    for copy in misc:
        copy.wait()
    ocean = c == 1
    wet[...] = jnp.where(ocean, weti[...].astype(F32), 1.0)
    rate[...] = rate[...] * wet[...]
    matrix = jnp.concatenate([ops[...], jnp.zeros((lev, 128 - lev), F32)], axis=1)
    high = matrix.astype(BF16).astype(F32)
    low = matrix - high
    lane = lane_ids((lev, 128))
    low80 = pltpu.roll(low, 80, 1)
    acat[...] = jnp.concatenate(
        [jnp.where(lane < 80, high, low80), jnp.where(lane < 32, low80, pltpu.roll(high, 32, 1))],
        axis=1,
    ).astype(BF16)
    acat16[...] = jnp.where(
        lane < flux,
        high,
        jnp.where(
            lane < 2 * flux,
            pltpu.roll(low, flux, 1),
            jnp.where(lane < 3 * flux, pltpu.roll(high, 2 * flux, 1), 0.0),
        ),
    ).astype(BF16)
    level = lax.broadcasted_iota(jnp.int32, (flux, 128), 0)
    scales = jnp.zeros((flux, 128), F32)
    gains = jnp.zeros((flux, 128), F32)
    for f in range(flux):
        scales = jnp.where(level == f, scale[0, f], scales)
        gains = jnp.where(level == f, gain[0, f], gains)

    for copy in state_copies:
        copy.wait()

    def group_of(box, t):
        return lambda r, g: box[t, r + 1, 8 * g : 8 * g + 8, :]

    parts = pack_edges(group_of(pad, 0), groups)
    for side in range(2):
        zpack[0, side] = jnp.concatenate(parts[side], axis=0)
    send_columns(zpack, hz, 0, hz_send, hz_recv)

    def column_of(t):
        wait_rows(pad, t, hx_recv)
        wait_columns(hz, t, hz_recv)
        packed = [[hz[t, side, 0:8], hz[t, side, 8:16]] for side in range(2)]
        for p in range(rows // 2):
            halves = []
            for r in (2 * p, 2 * p + 1):
                smooth = stencil(lambda i: pad[t, i], packed, groups, r)
                halves.append(
                    jnp.concatenate(split3(smooth, 80 - lev) + [jnp.zeros((16, 128), BF16)], axis=0)
                )
            both = jnp.dot(
                acat[...], jnp.concatenate(halves, axis=1), preferred_element_type=F32
            )
            ppre[2 * p] = both[:, :128]
            ppre[2 * p + 1] = both[:, 128:]

    column_of(0)
    for t in range(NSUB):
        final = t == NSUB - 1

        def keep(r, value):
            if final:
                last[r] = value
            else:
                pad[t + 1, r + 1] = value

        if t > 0:
            wait_rows(dpad, t - 1, dx_recv)
            wait_columns(dz, t - 1, dz_recv)
            dpacked = [[dz[t - 1, side]] for side in range(2)]
        for p in range(rows // 2):
            pair = [ppre[2 * p], ppre[2 * p + 1]]
            if t > 0:
                halves = []
                for r in (2 * p, 2 * p + 1):
                    smooth = stencil(lambda i: dpad[t - 1, i], dpacked, fgroups, r)
                    halves.append(jnp.concatenate(split3(smooth, 0), axis=0))
                both = jnp.dot(
                    acat16[:, : 3 * flux],
                    jnp.concatenate(halves, axis=1),
                    preferred_element_type=F32,
                )
                pair = [pair[0] + both[:, :128], pair[1] + both[:, 128:]]
            for i, r in enumerate((2 * p, 2 * p + 1)):
                es[t, r] = (jnp.tanh(scales * pair[i][:flux]) * wet[r : r + 1, :]).astype(BF16)
                keep(r, pair[i])
        mine = es.at[t]
        box = exs[t]
        remote(nxt, mine, box.at[0:rows], ex_send.at[t, 0], ex_recv.at[t, 0], over_next)
        remote(prev, mine, box.at[2 * rows : 3 * rows], ex_send.at[t, 2], ex_recv.at[t, 2], over_prev)
        remote(None, mine, box.at[rows : 2 * rows], ex_send.at[t, 1], ex_recv.at[t, 1], over)

        if final:
            rest = [
                pltpu.make_async_copy(
                    last.at[r, flux:], out.at[0, flux:, r, :], out_sem.at[0, r]
                )
                for r in range(rows)
            ]
            for copy in rest:
                copy.start()
        else:
            send_rows(pad.at[t + 1, 1], pad.at[t + 1, rows], pad, t + 1, hx_send, hx_recv)
            parts = pack_edges(group_of(pad, t + 1), groups)
            for side in range(2):
                zpack[t + 1, side] = jnp.concatenate(parts[side], axis=0)
            send_columns(zpack, hz, t + 1, hz_send, hz_recv)

        if t == 0:
            tile_copy.wait()
        receive(prev, box.at[0:rows], ex_recv.at[t, 0], over_prev)
        receive(None, box.at[rows : 2 * rows], ex_recv.at[t, 1], over)
        receive(nxt, box.at[2 * rows : 3 * rows], ex_recv.at[t, 2], over_next)
        for p in range(rows // 2):
            picked, weights = [], []
            for r in (2 * p, 2 * p + 1):
                chosen = []
                for k in range(depth):
                    index = jnp.where(k < count[0, 0, r], source[0, k, 0, r], 3 * rows)
                    chosen.append(box[index])
                picked.append(jnp.concatenate(chosen, axis=1))
                weights.append(w[r].reshape(depth * 128, 128))
            both = jnp.dot(
                jnp.concatenate(picked, axis=0),
                jnp.concatenate(weights, axis=1),
                preferred_element_type=F32,
            )
            for i, r in enumerate((2 * p, 2 * p + 1)):
                value = gains * wet[r : r + 1, :] * both[i * flux : (i + 1) * flux, i * 128 : (i + 1) * 128]
                if final:
                    last[r, 0:flux] += value
                else:
                    dpad[t, r + 1] = value
        if final:
            top = [
                pltpu.make_async_copy(
                    last.at[r, 0:flux], out.at[0, 0:flux, r, :], out_sem.at[1, r]
                )
                for r in range(rows)
            ]
            for copy in top:
                copy.start()
        else:
            send_rows(dpad.at[t, 1], dpad.at[t, rows], dpad, t, dx_send, dx_recv)
            parts = pack_edges(group_of(dpad, t), fgroups)
            for side in range(2):
                dzpack[t, side] = parts[side][0]
            send_columns(dzpack, dz, t, dz_send, dz_recv)
            column_of(t + 1)

    for flag, copy in sent:
        when(flag, copy.wait_send)
    for copy in rest + top:
        copy.wait()


def on_device(*args):
    fields, export_scale, tile_source = args[0], args[4], args[6]
    _, lev, rows, width = fields.shape
    flux, depth = export_scale.shape[1], tile_source.shape[3]
    dma = pltpu.SemaphoreType.DMA
    any_ = pl.BlockSpec(memory_space=pl.ANY)
    smem = pl.BlockSpec(memory_space=pltpu.SMEM)
    vmem = pltpu.VMEM
    box = vmem((3 * rows + 1, flux, width), BF16)
    return pl.pallas_call(
        functools.partial(kernel, (lev, rows, flux, depth)),
        out_shape=jax.ShapeDtypeStruct(fields.shape, F32),
        in_specs=[any_, any_, any_, any_, smem, smem, smem, smem, any_],
        out_specs=any_,
        scratch_shapes=[
            vmem((NSUB, rows + 2, lev, width), F32),
            vmem((NSUB - 1, rows + 2, flux, width), F32),
            vmem((NSUB, 2, 16, width), F32),
            vmem((NSUB - 1, 2, 8, width), F32),
            box,
            box,
            box,
            box,
            vmem((NSUB, rows, flux, width), BF16),
            vmem((rows, lev, width), F32),
            vmem((rows, lev, width), F32),
            vmem((NSUB, 2, 16, width), F32),
            vmem((NSUB - 1, 2, 8, width), F32),
            vmem((rows, depth, width, width), BF16),
            vmem((rows, width), F32),
            vmem((rows, width), jnp.int32),
            vmem((rows, width), F32),
            vmem((lev, lev), F32),
            vmem((lev, 256), BF16),
            vmem((lev, 128), BF16),
            dma((rows,)),
            dma((4,)),
            dma((2, rows)),
            dma((NSUB, 2)),
            dma((NSUB, 2)),
            dma((NSUB, 2)),
            dma((NSUB, 2)),
            dma((NSUB - 1, 2)),
            dma((NSUB - 1, 2)),
            dma((NSUB - 1, 2)),
            dma((NSUB - 1, 2)),
            dma((NSUB, 3)),
            dma((NSUB, 3)),
        ],
        compiler_params=pltpu.CompilerParams(
            collective_id=0, has_side_effects=True, vmem_limit_bytes=56 * 1024 * 1024
        ),
        name="coupled",
    )(*args[:6], jnp.transpose(args[6], (0, 3, 2, 1)), jnp.transpose(args[7], (0, 2, 1)), args[8])


def solution(mesh):
    in_specs = (
        P("comp", None, "gx", "gz"),
        P("comp", "gx", "gz"),
        P("gx", "gz"),
        P("comp", None, None),
        P("comp", None),
        P("comp", None),
        P("comp", "gx", "gz", None),
        P("comp", "gx", "gz"),
        P("comp", "gx", "gz", None, None, None),
    )
    out_specs = P("comp", None, "gx", "gz")
    return jax.shard_map(
        on_device, mesh=mesh, in_specs=in_specs, out_specs=out_specs, check_vma=False
    )
```

time: 520 us -> 48.7 us (0.09)
  the two profiles are of different devices: /device:TPU:134 before, /device:TPU:387 now
where the time goes in v1:
time: 48.7 us; the launch traced here: 48.5 us
  Pallas kernels  46.5 us (95%)
  local copies, waits for them, and re-layouts  1.92 us (4%)
    pallas_call x1, Pallas kernels, on_device(): pl.pallas_call(functools.partial(kernel, (lev, rows, flux, depth)), out_s...  46.5 us
    unnamed x1, local copies, waits for them, and re-layouts  1.92 us

profile of v1, /device:TPU:387, one launch (start us, length us, event | category | flops | bytes accessed | tf_op | source)
XLA Modules:
  0.0 48.5 jit_solution(4705528680639382175)
XLA Ops:
  0.0 46.5 %coupled.1 = f32[1,72,16,128]{3,2,1,0:T(8,128)} custom-call(f32[1,72,16,128]{3,2,1,0:T(8,128)} %fields.1, f32[1,16,128]{2,1,0:T(8,128)} %diff.1, s32[16,128]{1,0:T(8,128)} %wetm.1, f32[1,72,72]{2,1,0:T(8,128)} %op.1, f32[1,16]{1,0:T(1,128)} %scale.1, f32[1,16]{1,0:T(1,128)} %gain.1, s32[1,3,1,16]{3,2,1,0:T(1,128)} %bitcast.2, s32[1,1,16]{2,1,0:T(1,128)} %bitcast.3, ...), custom_call_target="tpu_custom_call" | custom-call | tf_op jit(solution)/shard_map/coupled/pallas_call | solution.py:405
  46.5 1.9 %copy.11 = f32[1,72,16,128]{3,2,1,0:T(8,128)} copy(f32[1,72,16,128]{3,2,1,0:T(8,128)} %coupled.1) | data formatting | bytes 1179648

commit v2 on v0

v2 whole, which is shorter than its diff:
```python
import functools

import jax
import jax.numpy as jnp
from jax import lax
from jax.experimental import pallas as pl
from jax.experimental.pallas import tpu as pltpu
from jax.sharding import PartitionSpec as P

NSUB = 4
MESH = pl.DeviceIdType.MESH
F32 = jnp.float32
BF16 = jnp.bfloat16


def lane_ids(shape):
    return lax.broadcasted_iota(jnp.int32, shape, 1)


def split3(value, pad):
    if pad:
        value = jnp.concatenate([value, jnp.zeros((pad, value.shape[1]), F32)], axis=0)
    high = value.astype(BF16)
    low = (value - high.astype(F32)).astype(BF16)
    return [high, high, low]


def place(group, row):
    return group // 4, 32 * (group % 4) + 2 * row


def kernel(dims, fields, diff, wetm, op, scale, gain, source, count, tiles, out, *scratch):
    lev, rows, flux, depth = dims
    (pad, dpad, hz, cp, rp, ppre, last, zpack, cpack, rpack, dsplit, w, wedge, wside, wcol, wcols, wd) = scratch[:17]
    (rate, weti, wet, wetn, wets, gw, ops, acat, acat16) = scratch[17:26]
    exs, ess = scratch[26:30], scratch[30:34]
    eff, eff_same, eff_over = scratch[34:37]
    local_sem, send_sem, recv_sem = scratch[37:40]
    groups, fgroups = lev // 8, flux // 8
    pairs = rows // 2
    c, gx, gz = lax.axis_index("comp"), lax.axis_index("gx"), lax.axis_index("gz")
    nx, nz = lax.axis_size("gx"), lax.axis_size("gz")
    prev, nxt, left, right = gx > 0, gx < nx - 1, gz > 0, gz < nz - 1
    prev2, nxt2 = gx > 1, gx < nx - 2

    def same(dx, dz):
        return (c, gx + dx, gz + dz)

    def over(dx, dz):
        return (1 - c, gx + dx, gz + dz)

    in_x = {-1: prev, 0: None, 1: nxt}

    def both(a, b):
        return b if a is None else a if b is None else jnp.logical_and(a, b)

    def when(flag, todo):
        if flag is None:
            todo()
        else:
            pl.when(flag)(todo)

    local = iter(range(100))

    def fetch(src, dst):
        copy = pltpu.make_async_copy(src, dst, local_sem.at[next(local)])
        copy.start()
        return copy

    state_copies = [fetch(fields.at[0, :, r, :], pad.at[0, r + 1]) for r in range(rows)]
    misc = [fetch(op.at[0], ops), fetch(diff.at[0], rate), fetch(wetm, weti)]
    tile_copy = fetch(tiles.at[0, :, 0], w)

    zeros_w = jnp.zeros((depth, 128, 128), BF16)
    zeros_ex = jnp.zeros((rows, flux, 128), BF16)
    no_source = jnp.concatenate([jnp.zeros((128, 128), BF16), jnp.full((16, 128), -1.0, BF16)], axis=0)

    def blank(flag, x_side):
        @pl.when(jnp.logical_not(flag))
        def _():
            edge = 0 if x_side == 0 else rows + 1
            pad[:, edge] = jnp.zeros((NSUB, lev, 128), F32)
            for ref in exs:
                ref[2 * rows * x_side : 2 * rows * x_side + rows] = zeros_ex
            wedge[x_side] = zeros_w
            wside[x_side] = zeros_w
            wcols[2 * x_side] = no_source
            wetn[x_side] = jnp.zeros((8, 128), jnp.int32)
            cp[:, 2 * x_side] = jnp.zeros((NSUB - 1, 2, 8, 128), F32)
            for k in range(8):
                eff_same[x_side, k] = -1
                eff_over[x_side, k] = -1

    blank(prev, 0)
    blank(nxt, 1)
    for x_side, flag in ((0, prev2), (1, nxt2)):

        @pl.when(jnp.logical_not(flag))
        def _():
            rp[:, x_side] = jnp.zeros((NSUB - 1, flux, 128), F32)

    for side, flag in ((0, left), (1, right)):

        @pl.when(jnp.logical_not(flag))
        def _():
            hz[:, side] = jnp.zeros((NSUB, 24, 128), F32)
            cp[:, :, side] = jnp.zeros((NSUB - 1, 3, 8, 128), F32)
            wets[side] = jnp.zeros((rows, 128), jnp.int32)

    for ref in exs:
        ref[3 * rows] = jnp.zeros((flux, 128), BF16)
    for ref in ess:
        ref[rows] = jnp.zeros((flux, 128), BF16)

    barrier = pltpu.get_barrier_semaphore()
    peers = [(None, over(0, 0))]
    peers += [(f, over(dx, 0)) for f, dx in ((prev, -1), (nxt, 1), (prev2, -2), (nxt2, 2))]
    peers += [(f, same(dx, 0)) for f, dx in ((prev, -1), (nxt, 1))]
    peers += [(f, same(0, dz)) for f, dz in ((left, -1), (right, 1))]
    peers += [
        (both(in_x[dx], f), over(dx, dz)) for dx in (-1, 0, 1) for f, dz in ((left, -1), (right, 1))
    ]
    expected = jnp.int32(0)
    for flag, peer in peers:
        when(
            flag,
            lambda peer=peer: pl.semaphore_signal(
                barrier, inc=1, device_id=peer, device_id_type=MESH
            ),
        )
        expected = expected + (1 if flag is None else flag.astype(jnp.int32))

    for copy in misc:
        copy.wait()
    ocean = c == 1
    wet[...] = jnp.where(ocean, weti[...].astype(F32), 1.0)
    rate[...] = rate[...] * wet[...]
    matrix = jnp.concatenate([ops[...], jnp.zeros((lev, 128 - lev), F32)], axis=1)
    high = matrix.astype(BF16).astype(F32)
    low = matrix - high
    lane = lane_ids((lev, 128))
    low80 = pltpu.roll(low, 80, 1)
    acat[...] = jnp.concatenate(
        [jnp.where(lane < 80, high, low80), jnp.where(lane < 32, low80, pltpu.roll(high, 32, 1))],
        axis=1,
    ).astype(BF16)
    acat16[...] = jnp.where(
        lane < flux,
        high,
        jnp.where(
            lane < 2 * flux,
            pltpu.roll(low, flux, 1),
            jnp.where(lane < 3 * flux, pltpu.roll(high, 2 * flux, 1), 0.0),
        ),
    ).astype(BF16)
    level = lax.broadcasted_iota(jnp.int32, (flux, 128), 0)
    scales = jnp.zeros((flux, 128), F32)
    gains = jnp.zeros((flux, 128), F32)
    for f in range(flux):
        scales = jnp.where(level == f, scale[0, f], scales)
        gains = jnp.where(level == f, gain[0, f], gains)

    def source_of(r, k):
        return jnp.where(k < count[0, 0, r], source[0, k, 0, r], -1)

    lane8 = lane_ids((8, 128))
    index = jnp.full((8, 128), -1, jnp.int32)
    for k in range(depth):
        for r in range(rows):
            index = jnp.where(lane8 // 2 == k * rows + r, source_of(r, k), index)
    index = index.astype(F32)
    for k in range(8):
        eff[k] = source_of(0 if k < 4 else rows - 1, k % 4) if k % 4 < depth else -1

    for copy in state_copies:
        copy.wait()

    def pack_edges(t):
        parts = [None] * 3
        for r in range(rows):
            for g in range(groups):
                slot, at = place(g, r)
                moved = pltpu.roll(pad[t, r + 1, 8 * g : 8 * g + 8, :], at + 1, 1)
                old = parts[slot]
                parts[slot] = moved if old is None else jnp.where(lane8 // 2 == at // 2, moved, old)
        zpack[t] = jnp.concatenate(parts, axis=0)

    pack_edges(0)

    pl.semaphore_wait(barrier, expected)

    ids = {}
    sent = []

    def remote(key, flag, src, dst, peer):
        at = ids.setdefault(key, len(ids))
        copy = pltpu.make_async_remote_copy(
            src_ref=src,
            dst_ref=dst,
            send_sem=send_sem.at[at],
            recv_sem=recv_sem.at[at],
            device_id=peer,
            device_id_type=MESH,
        )
        when(flag, copy.start)
        sent.append((flag, copy))

    def receive(key, flag, dst):
        at = ids[key]
        copy = pltpu.make_async_remote_copy(
            src_ref=dst,
            dst_ref=dst,
            send_sem=send_sem.at[at],
            recv_sem=recv_sem.at[at],
            device_id=over(0, 0),
            device_id_type=MESH,
        )
        when(flag, copy.wait_recv)

    def send_rows(first, last_row, t):
        remote(("hx", t, 0), nxt, last_row, pad.at[t, 0], same(1, 0))
        remote(("hx", t, 1), prev, first, pad.at[t, rows + 1], same(-1, 0))

    def send_columns(t):
        remote(("hz", t, 0), right, zpack.at[t], hz.at[t, 0], same(0, 1))
        remote(("hz", t, 1), left, zpack.at[t], hz.at[t, 1], same(0, -1))

    send_rows(fields.at[0, :, 0, :], fields.at[0, :, rows - 1, :], 0)
    send_columns(0)
    first, final_row = tiles.at[0, 0, 0], tiles.at[0, rows - 1, 0]
    remote("ws1", prev, final_row, wside.at[1], over(-1, 0))
    remote("ws0", nxt, first, wside.at[0], over(1, 0))
    remote("es0", nxt, eff, eff_same.at[0], same(1, 0))
    remote("es1", prev, eff, eff_same.at[1], same(-1, 0))
    remote("eo0", nxt, eff, eff_over.at[0], over(1, 0))
    remote("eo1", prev, eff, eff_over.at[1], over(-1, 0))
    remote("wn0", nxt, wetm.at[rows - 8 : rows], wetn.at[0], same(1, 0))
    remote("wn1", prev, wetm.at[0:8], wetn.at[1], same(-1, 0))
    remote("wz0", right, wetm, wets.at[0], same(0, 1))
    remote("wz1", left, wetm, wets.at[1], same(0, -1))

    tile_copy.wait()
    lane128 = lane_ids((128, 128))
    packed = jnp.zeros((128, 128), BF16)
    for k in range(depth):
        for r in range(rows):
            at = 2 * (k * rows + r)
            packed = jnp.where(lane128 // 2 == at // 2, pltpu.roll(w[r, k], at + 1, 1), packed)
    wcol[0:128] = packed
    wcol[128:144] = jnp.concatenate([index, index], axis=0).astype(BF16)
    for dx in (-1, 0, 1):
        remote(("wc", 1 - dx), in_x[dx], wcol, wcols.at[1 - dx], over(dx, 0))
    remote("we0", nxt, final_row, wedge.at[0], same(1, 0))
    remote("we1", prev, first, wedge.at[1], same(-1, 0))

    def merged_edges(t):
        odd = lane_ids((24, 128)) % 2 == 1
        return jnp.where(odd, hz[t, 1], hz[t, 0])

    def stencil(load, edges, n_groups, r):
        here = load(r + 1)
        levels = 8 * n_groups
        lane = lane_ids((levels, 128))
        moved = []
        for g in range(n_groups):
            slot, at = place(g, r)
            moved.append(pltpu.roll(edges[8 * slot : 8 * slot + 8], (127 - at) % 128, 1))
        beyond = jnp.concatenate(moved, axis=0)
        before = pltpu.roll(jnp.where(lane == 127, beyond, here), 1, 1)
        after = pltpu.roll(jnp.where(lane == 0, beyond, here), 127, 1)
        beside = load(r + 2) + load(r) + after + before
        return here + rate[r : r + 1, :] * (beside - 4.0 * here)

    def column_of(t, edges, some):
        for p in some:
            halves = []
            for r in (2 * p, 2 * p + 1):
                smooth = stencil(lambda i: pad[t, i], edges, groups, r)
                halves.append(
                    jnp.concatenate(split3(smooth, 80 - lev) + [jnp.zeros((16, 128), BF16)], axis=0)
                )
            product = jnp.dot(
                acat[...], jnp.concatenate(halves, axis=1), preferred_element_type=F32
            )
            ppre[2 * p] = product[:, :128]
            ppre[2 * p + 1] = product[:, 128:]

    def column_inner(t):
        receive(("hz", t, 0), left, hz.at[t, 0])
        receive(("hz", t, 1), right, hz.at[t, 1])
        column_of(t, merged_edges(t), range(1, pairs - 1))

    def column_outer(t):
        receive(("hx", t, 0), prev, pad.at[t, 0])
        receive(("hx", t, 1), nxt, pad.at[t, rows + 1])
        column_of(t, merged_edges(t), (0, pairs - 1))

    def pair_product(picks, weights):
        product = jnp.dot(
            jnp.concatenate([jnp.concatenate(row, axis=1) for row in picks], axis=0),
            jnp.concatenate([tile.reshape(depth * 128, 128) for tile in weights], axis=1),
            preferred_element_type=F32,
        )
        return product[:flux, :128], product[flux:, 128:]

    column_inner(0)
    column_outer(0)
    for t in range(NSUB):
        final = t == NSUB - 1
        col, at_col = (last, ()) if final else (pad, (t + 1,))

        def col_at(r):
            return (*at_col, r + (0 if final else 1))

        box, mine = exs[t], ess[t]
        for p in range(pairs):
            pair = [ppre[2 * p, 0:flux], ppre[2 * p + 1, 0:flux]]
            if t > 0:
                halves = []
                for r in (2 * p, 2 * p + 1):
                    smooth = stencil(lambda i: dpad[t - 1, i], dedges, fgroups, r)
                    halves.append(jnp.concatenate(split3(smooth, 0), axis=0))
                halves = jnp.concatenate(halves, axis=1)
                dsplit[p] = halves
                product = jnp.dot(acat16[0:flux, : 3 * flux], halves, preferred_element_type=F32)
                pair = [pair[0] + product[:, :128], pair[1] + product[:, 128:]]
            for i, r in enumerate((2 * p, 2 * p + 1)):
                mine[r] = (jnp.tanh(scales * pair[i]) * wet[r : r + 1, :]).astype(BF16)
                col[(*col_at(r), slice(0, flux))] = pair[i]
        block = mine.at[0:rows]
        remote(("ex", t, 0), nxt, block, box.at[0:rows], over(1, 0))
        remote(("ex", t, 2), prev, block, box.at[2 * rows : 3 * rows], over(-1, 0))
        remote(("ex", t, 1), None, block, box.at[rows : 2 * rows], over(0, 0))

        if not final:
            if t == 0:
                receive("ws0", prev, wside.at[0])
                receive("ws1", nxt, wside.at[1])
                receive("eo0", prev, eff_over.at[0])
                receive("eo1", nxt, eff_over.at[1])
            picks = [[], []]
            for k in range(depth):
                above, below = eff_over[0, k], eff_over[1, 4 + k]
                picks[0].append(mine[jnp.where(above >= 2 * rows, above - 2 * rows, rows)])
                picks[1].append(
                    mine[jnp.where(jnp.logical_and(below >= 0, below < rows), below, rows)]
                )
            parts = pair_product(picks, (wside[0], wside[1]))
            rpack[t, 0] = parts[0]
            rpack[t, 1] = parts[1]
            remote(("rp", t, 1), prev2, rpack.at[t, 0], rp.at[t, 1], over(-2, 0))
            remote(("rp", t, 0), nxt2, rpack.at[t, 1], rp.at[t, 0], over(2, 0))
            if t == 0:
                for dx in (-1, 0, 1):
                    receive(("wc", dx + 1), in_x[dx], wcols.at[dx + 1])
                    column, tag = wcols[dx + 1, 0:128], wcols[dx + 1, 128:144].astype(F32)[0:1]
                    for s in range(rows):
                        chosen = jnp.where(tag == float(rows * (1 - dx) + s), 1.0, 0.0).astype(BF16)
                        wd[s, :, 128 * (dx + 1) : 128 * (dx + 2)] = column * chosen
            product = jnp.dot(
                jnp.concatenate([mine[s] for s in range(rows)], axis=1),
                wd[...].reshape(rows * 128, 3 * 128),
                preferred_element_type=F32,
            )
            for dx in (-1, 0, 1):
                value = product[:, 128 * (dx + 1) : 128 * (dx + 2)]
                total = value
                for k in range(1, depth):
                    total = total + pltpu.roll(value, 128 - 2 * rows * k, 1)
                cpack[t, dx + 1] = jnp.where(
                    lane8 < 2 * rows, total[0:8], pltpu.roll(total[8:16], 2 * rows, 1)
                )
                for side, flag, dz in ((0, right, 1), (1, left, -1)):
                    remote(
                        ("cp", t, 1 - dx, side),
                        both(in_x[dx], flag),
                        cpack.at[t, dx + 1],
                        cp.at[t, 1 - dx, side],
                        over(dx, dz),
                    )

        if t > 0:
            for p in range(pairs):
                product = jnp.dot(
                    acat16[flux:, : 3 * flux], dsplit[p], preferred_element_type=F32
                )
                for i, r in enumerate((2 * p, 2 * p + 1)):
                    col[(*col_at(r), slice(flux, lev))] = (
                        ppre[r, flux:] + product[:, i * 128 : (i + 1) * 128]
                    )
        else:
            for r in range(rows):
                col[(*col_at(r), slice(flux, lev))] = ppre[r, flux:]

        if final:
            rest = [fetch(last.at[r, flux:], out.at[0, flux:, r, :]) for r in range(rows)]
        else:
            send_rows(pad.at[t + 1, 1], pad.at[t + 1, rows], t + 1)
            pack_edges(t + 1)
            send_columns(t + 1)
            column_inner(t + 1)

        receive(("ex", t, 1), None, box.at[rows : 2 * rows])
        receive(("ex", t, 0), prev, box.at[0:rows])
        receive(("ex", t, 2), nxt, box.at[2 * rows : 3 * rows])
        for p in range(pairs):
            picks = [[], []]
            for i in range(2):
                for k in range(depth):
                    at = source_of(2 * p + i, k)
                    picks[i].append(box[jnp.where(at >= 0, at, 3 * rows)])
            parts = pair_product(picks, (w[2 * p], w[2 * p + 1]))
            for i, r in enumerate((2 * p, 2 * p + 1)):
                value = gains * wet[r : r + 1, :] * parts[i]
                if final:
                    last[r, 0:flux] += value
                else:
                    dpad[t, r + 1] = value
        if final:
            top = [fetch(last.at[r, 0:flux], out.at[0, 0:flux, r, :]) for r in range(rows)]
        else:
            if t == 0:
                receive("es0", prev, eff_same.at[0])
                receive("es1", nxt, eff_same.at[1])
                receive("we0", prev, wedge.at[0])
                receive("we1", nxt, wedge.at[1])
                receive("wn0", prev, wetn.at[0])
                receive("wn1", nxt, wetn.at[1])
                receive("wz0", left, wets.at[0])
                receive("wz1", right, wets.at[1])
                wet_up = jnp.where(ocean, wetn[0, 7:8].astype(F32), 1.0)
                wet_down = jnp.where(ocean, wetn[1, 0:1].astype(F32), 1.0)
                beside = jnp.zeros((8, 128), F32)
                for r in range(rows):
                    for side, have in ((0, 127), (1, 0)):
                        at = 2 * r + side
                        cells = jnp.broadcast_to(wets[side, r : r + 1].astype(F32), (8, 128))
                        beside = jnp.where(
                            lane8 == at, pltpu.roll(cells, (at - have) % 128, 1), beside
                        )
                beside = jnp.where(ocean, beside, 1.0)
                gw[...] = jnp.where(
                    lane8 < 2 * rows,
                    beside * gains[0:8],
                    pltpu.roll(beside, 2 * rows, 1) * gains[8:16],
                )
            picks = [[], []]
            for k in range(depth):
                above, below = eff_same[0, 4 + k], eff_same[1, k]
                picks[0].append(box[jnp.where(above >= rows, above - rows, 3 * rows)])
                picks[1].append(
                    box[
                        jnp.where(
                            jnp.logical_and(below >= 0, below < 2 * rows), below + rows, 3 * rows
                        )
                    ]
                )
            parts = pair_product(picks, (wedge[0], wedge[1]))
            receive(("rp", t, 0), prev2, rp.at[t, 0])
            receive(("rp", t, 1), nxt2, rp.at[t, 1])
            dpad[t, 0] = gains * wet_up * (parts[0] + rp[t, 0])
            dpad[t, rows + 1] = gains * wet_down * (parts[1] + rp[t, 1])
            for dx in (-1, 0, 1):
                receive(("cp", t, dx + 1, 0), both(in_x[dx], left), cp.at[t, dx + 1, 0])
                receive(("cp", t, dx + 1, 1), both(in_x[dx], right), cp.at[t, dx + 1, 1])
            dedges = gw[...] * jnp.where(
                lane8 % 2 == 1,
                cp[t, 0, 1] + cp[t, 1, 1] + cp[t, 2, 1],
                cp[t, 0, 0] + cp[t, 1, 0] + cp[t, 2, 0],
            )
            column_outer(t + 1)

    for flag, copy in sent:
        when(flag, copy.wait_send)
    for copy in rest + top:
        copy.wait()


def on_device(*args):
    fields, export_scale, tile_source = args[0], args[4], args[6]
    _, lev, rows, width = fields.shape
    flux, depth = export_scale.shape[1], tile_source.shape[3]
    dma = pltpu.SemaphoreType.DMA
    any_ = pl.BlockSpec(memory_space=pl.ANY)
    smem = pl.BlockSpec(memory_space=pltpu.SMEM)
    vmem = pltpu.VMEM
    box = vmem((3 * rows + 1, flux, width), BF16)
    mine = vmem((rows + 1, flux, width), BF16)
    return pl.pallas_call(
        functools.partial(kernel, (lev, rows, flux, depth)),
        out_shape=jax.ShapeDtypeStruct(fields.shape, F32),
        in_specs=[any_, any_, any_, any_, smem, smem, smem, smem, any_],
        out_specs=any_,
        scratch_shapes=[
            vmem((NSUB, rows + 2, lev, width), F32),
            vmem((NSUB - 1, rows + 2, flux, width), F32),
            vmem((NSUB, 2, 24, width), F32),
            vmem((NSUB - 1, 3, 2, 8, width), F32),
            vmem((NSUB - 1, 2, flux, width), F32),
            vmem((rows, lev, width), F32),
            vmem((rows, lev, width), F32),
            vmem((NSUB, 24, width), F32),
            vmem((NSUB - 1, 3, 8, width), F32),
            vmem((NSUB - 1, 2, flux, width), F32),
            vmem((rows // 2, 3 * flux, 2 * width), BF16),
            vmem((rows, depth, width, width), BF16),
            vmem((2, depth, width, width), BF16),
            vmem((2, depth, width, width), BF16),
            vmem((144, width), BF16),
            vmem((3, 144, width), BF16),
            vmem((rows, width, 3 * width), BF16),
            vmem((rows, width), F32),
            vmem((rows, width), jnp.int32),
            vmem((rows, width), F32),
            vmem((2, 8, width), jnp.int32),
            vmem((2, rows, width), jnp.int32),
            vmem((8, width), F32),
            vmem((lev, lev), F32),
            vmem((lev, 256), BF16),
            vmem((lev, 128), BF16),
            box,
            box,
            box,
            box,
            mine,
            mine,
            mine,
            mine,
            pltpu.SMEM((8,), jnp.int32),
            pltpu.SMEM((2, 8), jnp.int32),
            pltpu.SMEM((2, 8), jnp.int32),
            dma((52,)),
            dma((80,)),
            dma((80,)),
        ],
        compiler_params=pltpu.CompilerParams(
            collective_id=0, has_side_effects=True, vmem_limit_bytes=56 * 1024 * 1024
        ),
        name="coupled",
    )(*args[:6], jnp.transpose(args[6], (0, 3, 2, 1)), jnp.transpose(args[7], (0, 2, 1)), args[8])


def solution(mesh):
    in_specs = (
        P("comp", None, "gx", "gz"),
        P("comp", "gx", "gz"),
        P("gx", "gz"),
        P("comp", None, None),
        P("comp", None),
        P("comp", None),
        P("comp", "gx", "gz", None),
        P("comp", "gx", "gz"),
        P("comp", "gx", "gz", None, None, None),
    )
    out_specs = P("comp", None, "gx", "gz")
    return jax.shard_map(
        on_device, mesh=mesh, in_specs=in_specs, out_specs=out_specs, check_vma=False
    )
```

time: 520 us -> 43.5 us (0.08)
  the two profiles are of different devices: /device:TPU:134 before, /device:TPU:385 now
where the time goes in v2:
time: 43.5 us; the launch traced here: 43.3 us
  Pallas kernels  41.4 us (95%)
  local copies, waits for them, and re-layouts  1.92 us (4%)
    pallas_call x1, Pallas kernels, on_device(): pl.pallas_call(functools.partial(kernel, (lev, rows, flux, depth)), out_s...  41.4 us
    unnamed x1, local copies, waits for them, and re-layouts  1.92 us

profile of v2, /device:TPU:385, one launch (start us, length us, event | category | flops | bytes accessed | tf_op | source)
XLA Modules:
  0.0 43.3 jit_solution(11030110470621436080)
XLA Ops:
  0.0 41.4 %coupled.1 = f32[1,72,16,128]{3,2,1,0:T(8,128)} custom-call(f32[1,72,16,128]{3,2,1,0:T(8,128)} %fields.1, f32[1,16,128]{2,1,0:T(8,128)} %diff.1, s32[16,128]{1,0:T(8,128)} %wetm.1, f32[1,72,72]{2,1,0:T(8,128)} %op.1, f32[1,16]{1,0:T(1,128)} %scale.1, f32[1,16]{1,0:T(1,128)} %gain.1, s32[1,3,1,16]{3,2,1,0:T(1,128)} %bitcast.2, s32[1,1,16]{2,1,0:T(1,128)} %bitcast.3, ...), custom_call_target="tpu_custom_call" | custom-call | tf_op jit(solution)/shard_map/coupled/pallas_call | solution.py:489
  41.4 1.9 %copy.11 = f32[1,72,16,128]{3,2,1,0:T(8,128)} copy(f32[1,72,16,128]{3,2,1,0:T(8,128)} %coupled.1) | data formatting | bytes 1179648

commit v3 on v2

--- a/solution.py
+++ b/solution.py
@@ -29,13 +29,14 @@
     return group // 4, 32 * (group % 4) + 2 * row
 
 
-def kernel(dims, fields, diff, wetm, op, scale, gain, source, count, tiles, out, *scratch):
+def kernel(dims, fields, diff, wetm, op, scale_in, gain_in, source_in, count_in, tiles, out, *scratch):
     lev, rows, flux, depth = dims
-    (pad, dpad, hz, cp, rp, ppre, last, zpack, cpack, rpack, dsplit, w, wedge, wside, wcol, wcols, wd) = scratch[:17]
+    last = out
+    (pad, dpad, hz, cp, rp, ppre, hx, hxpack, zpack, cpack, rpack, dsplit, w, wedge, wcol, wcols, wd) = scratch[:17]
     (rate, weti, wet, wetn, wets, gw, ops, acat, acat16) = scratch[17:26]
     exs, ess = scratch[26:30], scratch[30:34]
-    eff, eff_same, eff_over = scratch[34:37]
-    local_sem, send_sem, recv_sem = scratch[37:40]
+    eff, eff_same, eff_over, scale, gain, source, count = scratch[34:41]
+    local_sem, send_sem, recv_sem = scratch[41:44]
     groups, fgroups = lev // 8, flux // 8
     pairs = rows // 2
     c, gx, gz = lax.axis_index("comp"), lax.axis_index("gx"), lax.axis_index("gz")
@@ -67,10 +68,6 @@
         copy.start()
         return copy
 
-    state_copies = [fetch(fields.at[0, :, r, :], pad.at[0, r + 1]) for r in range(rows)]
-    misc = [fetch(op.at[0], ops), fetch(diff.at[0], rate), fetch(wetm, weti)]
-    tile_copy = fetch(tiles.at[0, :, 0], w)
-
     zeros_w = jnp.zeros((depth, 128, 128), BF16)
     zeros_ex = jnp.zeros((rows, flux, 128), BF16)
     no_source = jnp.concatenate([jnp.zeros((128, 128), BF16), jnp.full((16, 128), -1.0, BF16)], axis=0)
@@ -78,12 +75,10 @@
     def blank(flag, x_side):
         @pl.when(jnp.logical_not(flag))
         def _():
-            edge = 0 if x_side == 0 else rows + 1
-            pad[:, edge] = jnp.zeros((NSUB, lev, 128), F32)
+            hx[:, x_side] = jnp.zeros((NSUB, 80, 128), BF16)
             for ref in exs:
                 ref[2 * rows * x_side : 2 * rows * x_side + rows] = zeros_ex
             wedge[x_side] = zeros_w
-            wside[x_side] = zeros_w
             wcols[2 * x_side] = no_source
             wetn[x_side] = jnp.zeros((8, 128), jnp.int32)
             cp[:, 2 * x_side] = jnp.zeros((NSUB - 1, 2, 8, 128), F32)
@@ -97,7 +92,7 @@
 
         @pl.when(jnp.logical_not(flag))
         def _():
-            rp[:, x_side] = jnp.zeros((NSUB - 1, flux, 128), F32)
+            rp[:, x_side] = jnp.zeros((NSUB - 1, depth, flux, 128), BF16)
 
     for side, flag in ((0, left), (1, right)):
 
@@ -129,6 +124,11 @@
             ),
         )
         expected = expected + (1 if flag is None else flag.astype(jnp.int32))
+
+    misc = [fetch(op.at[0], ops), fetch(diff.at[0], rate), fetch(wetm, weti)]
+    misc += [fetch(scale_in, scale), fetch(gain_in, gain), fetch(source_in, source), fetch(count_in, count)]
+    state_copies = [fetch(fields.at[0, :, r, :], pad.at[0, r + 1]) for r in range(rows)]
+    tile_copy = fetch(tiles.at[0, :, 0], w)
 
     for copy in misc:
         copy.wait()
@@ -185,6 +185,11 @@
                 parts[slot] = moved if old is None else jnp.where(lane8 // 2 == at // 2, moved, old)
         zpack[t] = jnp.concatenate(parts, axis=0)
 
+    def pack_rows(t):
+        for i, at in enumerate((rows, 1)):
+            hxpack[t, i] = jnp.concatenate([pad[t, at], jnp.zeros((80 - lev, 128), F32)], axis=0).astype(BF16)
+
+    pack_rows(0)
     pack_edges(0)
 
     pl.semaphore_wait(barrier, expected)
@@ -217,19 +222,17 @@
         )
         when(flag, copy.wait_recv)
 
-    def send_rows(first, last_row, t):
-        remote(("hx", t, 0), nxt, last_row, pad.at[t, 0], same(1, 0))
-        remote(("hx", t, 1), prev, first, pad.at[t, rows + 1], same(-1, 0))
+    def send_rows(t):
+        remote(("hx", t, 0), nxt, hxpack.at[t, 0], hx.at[t, 0], same(1, 0))
+        remote(("hx", t, 1), prev, hxpack.at[t, 1], hx.at[t, 1], same(-1, 0))
 
     def send_columns(t):
         remote(("hz", t, 0), right, zpack.at[t], hz.at[t, 0], same(0, 1))
         remote(("hz", t, 1), left, zpack.at[t], hz.at[t, 1], same(0, -1))
 
-    send_rows(fields.at[0, :, 0, :], fields.at[0, :, rows - 1, :], 0)
+    send_rows(0)
     send_columns(0)
     first, final_row = tiles.at[0, 0, 0], tiles.at[0, rows - 1, 0]
-    remote("ws1", prev, final_row, wside.at[1], over(-1, 0))
-    remote("ws0", nxt, first, wside.at[0], over(1, 0))
     remote("es0", nxt, eff, eff_same.at[0], same(1, 0))
     remote("es1", prev, eff, eff_same.at[1], same(-1, 0))
     remote("eo0", nxt, eff, eff_over.at[0], over(1, 0))
@@ -272,10 +275,15 @@
         return here + rate[r : r + 1, :] * (beside - 4.0 * here)
 
     def column_of(t, edges, some):
+        def row_of(i):
+            if i in (0, rows + 1):
+                return hx[t, min(i, 1)].astype(F32)[:lev]
+            return pad[t, i]
+
         for p in some:
             halves = []
             for r in (2 * p, 2 * p + 1):
-                smooth = stencil(lambda i: pad[t, i], edges, groups, r)
+                smooth = stencil(row_of, edges, groups, r)
                 halves.append(
                     jnp.concatenate(split3(smooth, 80 - lev) + [jnp.zeros((16, 128), BF16)], axis=0)
                 )
@@ -291,8 +299,8 @@
         column_of(t, merged_edges(t), range(1, pairs - 1))
 
     def column_outer(t):
-        receive(("hx", t, 0), prev, pad.at[t, 0])
-        receive(("hx", t, 1), nxt, pad.at[t, rows + 1])
+        receive(("hx", t, 0), prev, hx.at[t, 0])
+        receive(("hx", t, 1), nxt, hx.at[t, 1])
         column_of(t, merged_edges(t), (0, pairs - 1))
 
     def pair_product(picks, weights):
@@ -302,6 +310,36 @@
             preferred_element_type=F32,
         )
         return product[:flux, :128], product[flux:, 128:]
+
+    def send_parts(t):
+        if t == 0:
+            for dx in (-1, 0, 1):
+                receive(("wc", dx + 1), in_x[dx], wcols.at[dx + 1])
+                column, tag = wcols[dx + 1, 0:128], wcols[dx + 1, 128:144].astype(F32)[0:1]
+                for s in range(rows):
+                    chosen = jnp.where(tag == float(rows * (1 - dx) + s), 1.0, 0.0).astype(BF16)
+                    wd[s, :, 128 * (dx + 1) : 128 * (dx + 2)] = column * chosen
+        product = jnp.dot(
+            jnp.concatenate([ess[t][s] for s in range(rows)], axis=1),
+            wd[...].reshape(rows * 128, 3 * 128),
+            preferred_element_type=F32,
+        )
+        for dx in (-1, 0, 1):
+            value = product[:, 128 * (dx + 1) : 128 * (dx + 2)]
+            total = value
+            for k in range(1, depth):
+                total = total + pltpu.roll(value, 128 - 2 * rows * k, 1)
+            cpack[t, dx + 1] = jnp.where(
+                lane8 < 2 * rows, total[0:8], pltpu.roll(total[8:16], 2 * rows, 1)
+            )
+            for side, flag, dz in ((0, right, 1), (1, left, -1)):
+                remote(
+                    ("cp", t, 1 - dx, side),
+                    both(in_x[dx], flag),
+                    cpack.at[t, dx + 1],
+                    cp.at[t, 1 - dx, side],
+                    over(dx, dz),
+                )
 
     column_inner(0)
     column_outer(0)
@@ -334,51 +372,17 @@
 
         if not final:
             if t == 0:
-                receive("ws0", prev, wside.at[0])
-                receive("ws1", nxt, wside.at[1])
                 receive("eo0", prev, eff_over.at[0])
                 receive("eo1", nxt, eff_over.at[1])
-            picks = [[], []]
             for k in range(depth):
                 above, below = eff_over[0, k], eff_over[1, 4 + k]
-                picks[0].append(mine[jnp.where(above >= 2 * rows, above - 2 * rows, rows)])
-                picks[1].append(
-                    mine[jnp.where(jnp.logical_and(below >= 0, below < rows), below, rows)]
-                )
-            parts = pair_product(picks, (wside[0], wside[1]))
-            rpack[t, 0] = parts[0]
-            rpack[t, 1] = parts[1]
+                rpack[t, 0, k] = mine[jnp.where(above >= 2 * rows, above - 2 * rows, rows)]
+                rpack[t, 1, k] = mine[jnp.where(jnp.logical_and(below >= 0, below < rows), below, rows)]
             remote(("rp", t, 1), prev2, rpack.at[t, 0], rp.at[t, 1], over(-2, 0))
             remote(("rp", t, 0), nxt2, rpack.at[t, 1], rp.at[t, 0], over(2, 0))
-            if t == 0:
-                for dx in (-1, 0, 1):
-                    receive(("wc", dx + 1), in_x[dx], wcols.at[dx + 1])
-                    column, tag = wcols[dx + 1, 0:128], wcols[dx + 1, 128:144].astype(F32)[0:1]
-                    for s in range(rows):
-                        chosen = jnp.where(tag == float(rows * (1 - dx) + s), 1.0, 0.0).astype(BF16)
-                        wd[s, :, 128 * (dx + 1) : 128 * (dx + 2)] = column * chosen
-            product = jnp.dot(
-                jnp.concatenate([mine[s] for s in range(rows)], axis=1),
-                wd[...].reshape(rows * 128, 3 * 128),
-                preferred_element_type=F32,
-            )
-            for dx in (-1, 0, 1):
-                value = product[:, 128 * (dx + 1) : 128 * (dx + 2)]
-                total = value
-                for k in range(1, depth):
-                    total = total + pltpu.roll(value, 128 - 2 * rows * k, 1)
-                cpack[t, dx + 1] = jnp.where(
-                    lane8 < 2 * rows, total[0:8], pltpu.roll(total[8:16], 2 * rows, 1)
-                )
-                for side, flag, dz in ((0, right, 1), (1, left, -1)):
-                    remote(
-                        ("cp", t, 1 - dx, side),
-                        both(in_x[dx], flag),
-                        cpack.at[t, dx + 1],
-                        cp.at[t, 1 - dx, side],
-                        over(dx, dz),
-                    )
-
+
+        if 0 < t < NSUB - 1:
+            send_parts(t)
         if t > 0:
             for p in range(pairs):
                 product = jnp.dot(
@@ -392,12 +396,13 @@
             for r in range(rows):
                 col[(*col_at(r), slice(flux, lev))] = ppre[r, flux:]
 
-        if final:
-            rest = [fetch(last.at[r, flux:], out.at[0, flux:, r, :]) for r in range(rows)]
-        else:
-            send_rows(pad.at[t + 1, 1], pad.at[t + 1, rows], t + 1)
+        if not final:
+            pack_rows(t + 1)
+            send_rows(t + 1)
             pack_edges(t + 1)
             send_columns(t + 1)
+            if t == 0:
+                send_parts(0)
             column_inner(t + 1)
 
         receive(("ex", t, 1), None, box.at[rows : 2 * rows])
@@ -416,9 +421,7 @@
                     last[r, 0:flux] += value
                 else:
                     dpad[t, r + 1] = value
-        if final:
-            top = [fetch(last.at[r, 0:flux], out.at[0, 0:flux, r, :]) for r in range(rows)]
-        else:
+        if not final:
             if t == 0:
                 receive("es0", prev, eff_same.at[0])
                 receive("es1", nxt, eff_same.at[1])
@@ -444,22 +447,18 @@
                     beside * gains[0:8],
                     pltpu.roll(beside, 2 * rows, 1) * gains[8:16],
                 )
+            receive(("rp", t, 0), prev2, rp.at[t, 0])
+            receive(("rp", t, 1), nxt2, rp.at[t, 1])
             picks = [[], []]
             for k in range(depth):
                 above, below = eff_same[0, 4 + k], eff_same[1, k]
-                picks[0].append(box[jnp.where(above >= rows, above - rows, 3 * rows)])
-                picks[1].append(
-                    box[
-                        jnp.where(
-                            jnp.logical_and(below >= 0, below < 2 * rows), below + rows, 3 * rows
-                        )
-                    ]
-                )
+                here = jnp.where(above >= rows, above - rows, 3 * rows)
+                picks[0].append(box[here] + rp[t, 0, k])
+                here = jnp.where(jnp.logical_and(below >= 0, below < 2 * rows), below + rows, 3 * rows)
+                picks[1].append(box[here] + rp[t, 1, k])
             parts = pair_product(picks, (wedge[0], wedge[1]))
-            receive(("rp", t, 0), prev2, rp.at[t, 0])
-            receive(("rp", t, 1), nxt2, rp.at[t, 1])
-            dpad[t, 0] = gains * wet_up * (parts[0] + rp[t, 0])
-            dpad[t, rows + 1] = gains * wet_down * (parts[1] + rp[t, 1])
+            dpad[t, 0] = gains * wet_up * parts[0]
+            dpad[t, rows + 1] = gains * wet_down * parts[1]
             for dx in (-1, 0, 1):
                 receive(("cp", t, dx + 1, 0), both(in_x[dx], left), cp.at[t, dx + 1, 0])
                 receive(("cp", t, dx + 1, 1), both(in_x[dx], right), cp.at[t, dx + 1, 1])
@@ -472,8 +471,6 @@
 
     for flag, copy in sent:
         when(flag, copy.wait_send)
-    for copy in rest + top:
-        copy.wait()
 
 
 def on_device(*args):
@@ -482,29 +479,28 @@
     flux, depth = export_scale.shape[1], tile_source.shape[3]
     dma = pltpu.SemaphoreType.DMA
     any_ = pl.BlockSpec(memory_space=pl.ANY)
-    smem = pl.BlockSpec(memory_space=pltpu.SMEM)
     vmem = pltpu.VMEM
     box = vmem((3 * rows + 1, flux, width), BF16)
     mine = vmem((rows + 1, flux, width), BF16)
-    return pl.pallas_call(
+    result = pl.pallas_call(
         functools.partial(kernel, (lev, rows, flux, depth)),
-        out_shape=jax.ShapeDtypeStruct(fields.shape, F32),
-        in_specs=[any_, any_, any_, any_, smem, smem, smem, smem, any_],
-        out_specs=any_,
+        out_shape=pltpu.VMEM((rows, lev, width), F32),
+        in_specs=[any_] * 9,
+        out_specs=pl.BlockSpec(memory_space=pltpu.VMEM),
         scratch_shapes=[
             vmem((NSUB, rows + 2, lev, width), F32),
             vmem((NSUB - 1, rows + 2, flux, width), F32),
             vmem((NSUB, 2, 24, width), F32),
             vmem((NSUB - 1, 3, 2, 8, width), F32),
-            vmem((NSUB - 1, 2, flux, width), F32),
+            vmem((NSUB - 1, 2, depth, flux, width), BF16),
             vmem((rows, lev, width), F32),
-            vmem((rows, lev, width), F32),
+            vmem((NSUB, 2, 80, width), BF16),
+            vmem((NSUB, 2, 80, width), BF16),
             vmem((NSUB, 24, width), F32),
             vmem((NSUB - 1, 3, 8, width), F32),
-            vmem((NSUB - 1, 2, flux, width), F32),
+            vmem((NSUB - 1, 2, depth, flux, width), BF16),
             vmem((rows // 2, 3 * flux, 2 * width), BF16),
             vmem((rows, depth, width, width), BF16),
-            vmem((2, depth, width, width), BF16),
             vmem((2, depth, width, width), BF16),
             vmem((144, width), BF16),
             vmem((3, 144, width), BF16),
@@ -529,7 +525,11 @@
             pltpu.SMEM((8,), jnp.int32),
             pltpu.SMEM((2, 8), jnp.int32),
             pltpu.SMEM((2, 8), jnp.int32),
-            dma((52,)),
+            pltpu.SMEM((1, flux), F32),
+            pltpu.SMEM((1, flux), F32),
+            pltpu.SMEM((1, depth, 1, rows), jnp.int32),
+            pltpu.SMEM((1, 1, rows), jnp.int32),
+            dma((24,)),
             dma((80,)),
             dma((80,)),
         ],
@@ -538,6 +538,7 @@
         ),
         name="coupled",
     )(*args[:6], jnp.transpose(args[6], (0, 3, 2, 1)), jnp.transpose(args[7], (0, 2, 1)), args[8])
+    return jnp.transpose(result, (1, 0, 2))[None]
 
 
 def solution(mesh):

time: 43.5 us -> 38.3 us (0.88)
  Pallas kernels: 41.4 us -> 37.2 us
  local copies, waits for them, and re-layouts: 1.92 us -> 0.92 us
    pallas_call x1, Pallas kernels: 41.4 us -> 37.2 us  [on_device(): pl.pallas_call(functools.partial(kernel, (lev, rows, flux, depth)), out_s...]
    unnamed x1 -> x0, local copies, waits for them, and re-layouts: 1.92 us -> none
    broadcast_in_dim x0 -> x1, local copies, waits for them, and re-layouts: none -> 0.92 us  [on_device(): return jnp.transpose(result, (1, 0, 2))[None]]
where the time goes in v3:
time: 38.3 us; the launch traced here: 38.2 us
  Pallas kernels  37.2 us (97%)
  local copies, waits for them, and re-layouts  0.92 us (2%)
    pallas_call x1, Pallas kernels, on_device(): pl.pallas_call(functools.partial(kernel, (lev, rows, flux, depth)), out_s...  37.2 us
    broadcast_in_dim x1, local copies, waits for them, and re-layouts, on_device(): return jnp.transpose(result, (1, 0, 2))[None]  0.92 us

profile of v3, /device:TPU:385, one launch (start us, length us, event | category | flops | bytes accessed | tf_op | source)
XLA Modules:
  0.0 38.2 jit_solution(13957319523905816694)
XLA Ops:
  0.0 37.2 %coupled.1 = f32[16,72,128]{2,1,0:T(8,128)S(1)} custom-call(f32[1,72,16,128]{3,2,1,0:T(8,128)} %fields.1, f32[1,16,128]{2,1,0:T(8,128)} %diff.1, s32[16,128]{1,0:T(8,128)} %wetm.1, f32[1,72,72]{2,1,0:T(8,128)} %op.1, f32[1,16]{1,0:T(1,128)} %scale_in.1, f32[1,16]{1,0:T(1,128)} %gain_in.1, s32[1,3,1,16]{3,2,1,0:T(1,128)} %bitcast.6, s32[1,1,16]{2,1,0:T(1,128)} %bitcast.7, ...), custom_call_target="tpu_custom_call" | custom-call | tf_op jit(solution)/shard_map/coupled/pallas_call | solution.py:485
  37.2 0.9 %copy.10 = f32[1,72,16,128]{3,2,1,0:T(8,128)} copy(f32[1,72,16,128]{3,1,2,0:T(8,128)S(1)} %bitcast.5) | data formatting | bytes 1179648 | tf_op jit(solution)/shard_map/broadcast_in_dim | solution.py:541

commit v4 on v3

--- a/solution.py
+++ b/solution.py
@@ -109,12 +109,9 @@
 
     barrier = pltpu.get_barrier_semaphore()
     peers = [(None, over(0, 0))]
-    peers += [(f, over(dx, 0)) for f, dx in ((prev, -1), (nxt, 1), (prev2, -2), (nxt2, 2))]
+    peers += [(f, over(dx, 0)) for f, dx in ((prev, -1), (nxt, 1))]
     peers += [(f, same(dx, 0)) for f, dx in ((prev, -1), (nxt, 1))]
     peers += [(f, same(0, dz)) for f, dz in ((left, -1), (right, 1))]
-    peers += [
-        (both(in_x[dx], f), over(dx, dz)) for dx in (-1, 0, 1) for f, dz in ((left, -1), (right, 1))
-    ]
     expected = jnp.int32(0)
     for flag, peer in peers:
         when(
@@ -311,27 +308,44 @@
         )
         return product[:flux, :128], product[flux:, 128:]
 
-    def send_parts(t):
-        if t == 0:
+    def spread_columns():
+        group = lane128 // (2 * rows)
+        group8 = lane8 // (2 * rows)
+        for dx in (-1, 0, 1):
+            receive(("wc", dx + 1), in_x[dx], wcols.at[dx + 1])
+        tags, columns = [], []
+        for k in range(depth):
+            tag = jnp.full((8, 128), -1.0, F32)
+            column = jnp.zeros((128, 128), BF16)
             for dx in (-1, 0, 1):
-                receive(("wc", dx + 1), in_x[dx], wcols.at[dx + 1])
-                column, tag = wcols[dx + 1, 0:128], wcols[dx + 1, 128:144].astype(F32)[0:1]
-                for s in range(rows):
-                    chosen = jnp.where(tag == float(rows * (1 - dx) + s), 1.0, 0.0).astype(BF16)
-                    wd[s, :, 128 * (dx + 1) : 128 * (dx + 2)] = column * chosen
-        product = jnp.dot(
-            jnp.concatenate([ess[t][s] for s in range(rows)], axis=1),
-            wd[...].reshape(rows * 128, 3 * 128),
+                shift = (2 * rows * (dx + 1 - k)) % 128
+                moved, own = wcols[dx + 1, 0:128], wcols[dx + 1, 128:144].astype(F32)[0:8]
+                if shift:
+                    moved, own = pltpu.roll(moved, shift, 1), pltpu.roll(own, shift, 1)
+                tag = jnp.where(group8 == dx + 1, own - float(rows * (1 - dx)), tag)
+                column = jnp.where(group == dx + 1, moved, column)
+            tags.append(tag[0:1])
+            columns.append(column)
+        for row in range(rows):
+            total = None
+            for k in range(depth):
+                term = columns[k] * jnp.where(tags[k] == float(row), 1.0, 0.0).astype(BF16)
+                total = term if total is None else total + term
+            wd[row] = total
+
+    def send_parts(t, exported):
+        value = jnp.dot(
+            jnp.concatenate(exported, axis=1),
+            wd[...].reshape(rows * 128, 128),
             preferred_element_type=F32,
         )
         for dx in (-1, 0, 1):
-            value = product[:, 128 * (dx + 1) : 128 * (dx + 2)]
-            total = value
-            for k in range(1, depth):
-                total = total + pltpu.roll(value, 128 - 2 * rows * k, 1)
-            cpack[t, dx + 1] = jnp.where(
-                lane8 < 2 * rows, total[0:8], pltpu.roll(total[8:16], 2 * rows, 1)
-            )
+            halves = []
+            for g in range(fgroups):
+                shift = (2 * rows * (g - dx - 1)) % 128
+                half = value[8 * g : 8 * g + 8]
+                halves.append(pltpu.roll(half, shift, 1) if shift else half)
+            cpack[t, dx + 1] = jnp.where(lane8 < 2 * rows, halves[0], halves[1])
             for side, flag, dz in ((0, right, 1), (1, left, -1)):
                 remote(
                     ("cp", t, 1 - dx, side),
@@ -350,7 +364,7 @@
         def col_at(r):
             return (*at_col, r + (0 if final else 1))
 
-        box, mine = exs[t], ess[t]
+        box, mine, exported = exs[t], ess[t], []
         for p in range(pairs):
             pair = [ppre[2 * p, 0:flux], ppre[2 * p + 1, 0:flux]]
             if t > 0:
@@ -363,13 +377,19 @@
                 product = jnp.dot(acat16[0:flux, : 3 * flux], halves, preferred_element_type=F32)
                 pair = [pair[0] + product[:, :128], pair[1] + product[:, 128:]]
             for i, r in enumerate((2 * p, 2 * p + 1)):
-                mine[r] = (jnp.tanh(scales * pair[i]) * wet[r : r + 1, :]).astype(BF16)
+                exported.append((jnp.tanh(scales * pair[i]) * wet[r : r + 1, :]).astype(BF16))
+                mine[r] = exported[r]
                 col[(*col_at(r), slice(0, flux))] = pair[i]
         block = mine.at[0:rows]
-        remote(("ex", t, 0), nxt, block, box.at[0:rows], over(1, 0))
-        remote(("ex", t, 2), prev, block, box.at[2 * rows : 3 * rows], over(-1, 0))
-        remote(("ex", t, 1), None, block, box.at[rows : 2 * rows], over(0, 0))
-
+
+        def send_exports():
+            remote(("ex", t, 0), nxt, block, box.at[0:rows], over(1, 0))
+            remote(("ex", t, 2), prev, block, box.at[2 * rows : 3 * rows], over(-1, 0))
+            remote(("ex", t, 1), None, block, box.at[rows : 2 * rows], over(0, 0))
+
+        send_exports()
+        if 0 < t < NSUB - 1:
+            send_parts(t, exported)
         if not final:
             if t == 0:
                 receive("eo0", prev, eff_over.at[0])
@@ -380,9 +400,6 @@
                 rpack[t, 1, k] = mine[jnp.where(jnp.logical_and(below >= 0, below < rows), below, rows)]
             remote(("rp", t, 1), prev2, rpack.at[t, 0], rp.at[t, 1], over(-2, 0))
             remote(("rp", t, 0), nxt2, rpack.at[t, 1], rp.at[t, 0], over(2, 0))
-
-        if 0 < t < NSUB - 1:
-            send_parts(t)
         if t > 0:
             for p in range(pairs):
                 product = jnp.dot(
@@ -402,7 +419,8 @@
             pack_edges(t + 1)
             send_columns(t + 1)
             if t == 0:
-                send_parts(0)
+                spread_columns()
+                send_parts(0, [mine[i] for i in range(rows)])
             column_inner(t + 1)
 
         receive(("ex", t, 1), None, box.at[rows : 2 * rows])
@@ -504,7 +522,7 @@
             vmem((2, depth, width, width), BF16),
             vmem((144, width), BF16),
             vmem((3, 144, width), BF16),
-            vmem((rows, width, 3 * width), BF16),
+            vmem((rows, width, width), BF16),
             vmem((rows, width), F32),
             vmem((rows, width), jnp.int32),
             vmem((rows, width), F32),

time: 38.3 us -> 37.6 us (0.982)
  Pallas kernels: 37.2 us -> 36.5 us
    pallas_call x1, Pallas kernels: 37.2 us -> 36.5 us  [on_device(): pl.pallas_call(functools.partial(kernel, (lev, rows, flux, depth)), out_s...]
where the time goes in v4:
time: 37.6 us; the launch traced here: 37.5 us
  Pallas kernels  36.5 us (97%)
  local copies, waits for them, and re-layouts  0.92 us (2%)
    pallas_call x1, Pallas kernels, on_device(): pl.pallas_call(functools.partial(kernel, (lev, rows, flux, depth)), out_s...  36.5 us
    broadcast_in_dim x1, local copies, waits for them, and re-layouts, on_device(): return jnp.transpose(result, (1, 0, 2))[None]  0.92 us

profile of v4, /device:TPU:385, one launch (start us, length us, event | category | flops | bytes accessed | tf_op | source)
XLA Modules:
  0.0 37.5 jit_solution(7549036777138216102)
XLA Ops:
  0.0 36.5 %coupled.1 = f32[16,72,128]{2,1,0:T(8,128)S(1)} custom-call(f32[1,72,16,128]{3,2,1,0:T(8,128)} %fields.1, f32[1,16,128]{2,1,0:T(8,128)} %diff.1, s32[16,128]{1,0:T(8,128)} %wetm.1, f32[1,72,72]{2,1,0:T(8,128)} %op.1, f32[1,16]{1,0:T(1,128)} %scale_in.1, f32[1,16]{1,0:T(1,128)} %gain_in.1, s32[1,3,1,16]{3,2,1,0:T(1,128)} %bitcast.6, s32[1,1,16]{2,1,0:T(1,128)} %bitcast.7, ...), custom_call_target="tpu_custom_call" | custom-call | tf_op jit(solution)/shard_map/coupled/pallas_call | solution.py:503
  36.5 0.9 %copy.10 = f32[1,72,16,128]{3,2,1,0:T(8,128)} copy(f32[1,72,16,128]{3,1,2,0:T(8,128)S(1)} %bitcast.5) | data formatting | bytes 1179648 | tf_op jit(solution)/shard_map/broadcast_in_dim | solution.py:559

commit v5 on v4

--- a/solution.py
+++ b/solution.py
@@ -35,8 +35,8 @@
     (pad, dpad, hz, cp, rp, ppre, hx, hxpack, zpack, cpack, rpack, dsplit, w, wedge, wcol, wcols, wd) = scratch[:17]
     (rate, weti, wet, wetn, wets, gw, ops, acat, acat16) = scratch[17:26]
     exs, ess = scratch[26:30], scratch[30:34]
-    eff, eff_same, eff_over, scale, gain, source, count = scratch[34:41]
-    local_sem, send_sem, recv_sem = scratch[41:44]
+    eff, eff_same, eff_over, scale, gain, source, count, chosen = scratch[34:42]
+    local_sem, send_sem, recv_sem = scratch[42:45]
     groups, fgroups = lev // 8, flux // 8
     pairs = rows // 2
     c, gx, gz = lax.axis_index("comp"), lax.axis_index("gx"), lax.axis_index("gz")
@@ -122,10 +122,118 @@
         )
         expected = expected + (1 if flag is None else flag.astype(jnp.int32))
 
+    state_copies = [fetch(fields.at[0, :, r, :], pad.at[0, r + 1]) for r in range(rows)]
+    sources = [fetch(source_in, source), fetch(count_in, count)]
     misc = [fetch(op.at[0], ops), fetch(diff.at[0], rate), fetch(wetm, weti)]
-    misc += [fetch(scale_in, scale), fetch(gain_in, gain), fetch(source_in, source), fetch(count_in, count)]
-    state_copies = [fetch(fields.at[0, :, r, :], pad.at[0, r + 1]) for r in range(rows)]
+    misc += [fetch(scale_in, scale), fetch(gain_in, gain)]
     tile_copy = fetch(tiles.at[0, :, 0], w)
+
+    for copy in state_copies:
+        copy.wait()
+    lane8 = lane_ids((8, 128))
+
+    def pack_edges(t):
+        parts = [None] * 3
+        for r in range(rows):
+            for g in range(groups):
+                slot, at = place(g, r)
+                moved = pltpu.roll(pad[t, r + 1, 8 * g : 8 * g + 8, :], at + 1, 1)
+                old = parts[slot]
+                parts[slot] = moved if old is None else jnp.where(lane8 // 2 == at // 2, moved, old)
+        zpack[t] = jnp.concatenate(parts, axis=0)
+
+    def pack_rows(t):
+        for i, at in enumerate((rows, 1)):
+            hxpack[t, i] = jnp.concatenate([pad[t, at], jnp.zeros((80 - lev, 128), F32)], axis=0).astype(BF16)
+
+    pack_rows(0)
+    pack_edges(0)
+
+    pl.semaphore_wait(barrier, expected)
+
+    ids = {}
+    sent = []
+
+    def remote(key, flag, src, dst, peer):
+        at = ids.setdefault(key, len(ids))
+        copy = pltpu.make_async_remote_copy(
+            src_ref=src,
+            dst_ref=dst,
+            send_sem=send_sem.at[at],
+            recv_sem=recv_sem.at[at],
+            device_id=peer,
+            device_id_type=MESH,
+        )
+        when(flag, copy.start)
+        sent.append((flag, copy))
+
+    def receive(key, flag, dst):
+        at = ids[key]
+        copy = pltpu.make_async_remote_copy(
+            src_ref=dst,
+            dst_ref=dst,
+            send_sem=send_sem.at[at],
+            recv_sem=recv_sem.at[at],
+            device_id=over(0, 0),
+            device_id_type=MESH,
+        )
+        when(flag, copy.wait_recv)
+
+    def send_rows(t):
+        remote(("hx", t, 0), nxt, hxpack.at[t, 0], hx.at[t, 0], same(1, 0))
+        remote(("hx", t, 1), prev, hxpack.at[t, 1], hx.at[t, 1], same(-1, 0))
+
+    def send_columns(t):
+        remote(("hz", t, 0), right, zpack.at[t], hz.at[t, 0], same(0, 1))
+        remote(("hz", t, 1), left, zpack.at[t], hz.at[t, 1], same(0, -1))
+
+    send_rows(0)
+    send_columns(0)
+
+    def send_tiles(part):
+        first, final_row = tiles.at[0, 0, 0], tiles.at[0, rows - 1, 0]
+        remote(("we", 0, part.start), nxt, final_row.at[part], wedge.at[0, part], same(1, 0))
+        remote(("we", 1, part.start), prev, first.at[part], wedge.at[1, part], same(-1, 0))
+
+    parts_of_k = (slice(0, depth),)
+
+    for copy in sources:
+        copy.wait()
+
+    def source_of(r, k):
+        return jnp.where(k < count[0, 0, r], source[0, k, 0, r], -1)
+
+    index = jnp.full((8, 128), -1, jnp.int32)
+    for k in range(depth):
+        for r in range(rows):
+            at = source_of(r, k)
+            chosen[depth * r + k] = jnp.where(at >= 0, at, 3 * rows)
+            index = jnp.where(lane8 // 2 == k * rows + r, at, index)
+    index = index.astype(F32)
+    for k in range(8):
+        eff[k] = source_of(0 if k < 4 else rows - 1, k % 4) if k % 4 < depth else -1
+
+    tile_copy.wait()
+    lane128 = lane_ids((128, 128))
+    packed = jnp.zeros((128, 128), BF16)
+    for k in range(depth):
+        for r in range(rows):
+            at = 2 * (k * rows + r)
+            packed = jnp.where(lane128 // 2 == at // 2, pltpu.roll(w[r, k], at + 1, 1), packed)
+    wcol[0:128] = packed
+    wcol[128:144] = jnp.concatenate([index, index], axis=0).astype(BF16)
+    for dx in (-1, 0, 1):
+        remote(("wc", 1 - dx), in_x[dx], wcol, wcols.at[1 - dx], over(dx, 0))
+    remote("es0", nxt, eff, eff_same.at[0], same(1, 0))
+    remote("es1", prev, eff, eff_same.at[1], same(-1, 0))
+    remote("eo0", nxt, eff, eff_over.at[0], over(1, 0))
+    remote("eo1", prev, eff, eff_over.at[1], over(-1, 0))
+    remote("wn0", nxt, wetm.at[rows - 8 : rows], wetn.at[0], same(1, 0))
+    remote("wn1", prev, wetm.at[0:8], wetn.at[1], same(-1, 0))
+    remote("wz0", right, wetm, wets.at[0], same(0, 1))
+    remote("wz1", left, wetm, wets.at[1], same(0, -1))
+
+    send_tiles(parts_of_k[0])
 
     for copy in misc:
         copy.wait()
@@ -157,101 +265,6 @@
         scales = jnp.where(level == f, scale[0, f], scales)
         gains = jnp.where(level == f, gain[0, f], gains)
 
-    def source_of(r, k):
-        return jnp.where(k < count[0, 0, r], source[0, k, 0, r], -1)
-
-    lane8 = lane_ids((8, 128))
-    index = jnp.full((8, 128), -1, jnp.int32)
-    for k in range(depth):
-        for r in range(rows):
-            index = jnp.where(lane8 // 2 == k * rows + r, source_of(r, k), index)
-    index = index.astype(F32)
-    for k in range(8):
-        eff[k] = source_of(0 if k < 4 else rows - 1, k % 4) if k % 4 < depth else -1
-
-    for copy in state_copies:
-        copy.wait()
-
-    def pack_edges(t):
-        parts = [None] * 3
-        for r in range(rows):
-            for g in range(groups):
-                slot, at = place(g, r)
-                moved = pltpu.roll(pad[t, r + 1, 8 * g : 8 * g + 8, :], at + 1, 1)
-                old = parts[slot]
-                parts[slot] = moved if old is None else jnp.where(lane8 // 2 == at // 2, moved, old)
-        zpack[t] = jnp.concatenate(parts, axis=0)
-
-    def pack_rows(t):
-        for i, at in enumerate((rows, 1)):
-            hxpack[t, i] = jnp.concatenate([pad[t, at], jnp.zeros((80 - lev, 128), F32)], axis=0).astype(BF16)
-
-    pack_rows(0)
-    pack_edges(0)
-
-    pl.semaphore_wait(barrier, expected)
-
-    ids = {}
-    sent = []
-
-    def remote(key, flag, src, dst, peer):
-        at = ids.setdefault(key, len(ids))
-        copy = pltpu.make_async_remote_copy(
-            src_ref=src,
-            dst_ref=dst,
-            send_sem=send_sem.at[at],
-            recv_sem=recv_sem.at[at],
-            device_id=peer,
-            device_id_type=MESH,
-        )
-        when(flag, copy.start)
-        sent.append((flag, copy))
-
-    def receive(key, flag, dst):
-        at = ids[key]
-        copy = pltpu.make_async_remote_copy(
-            src_ref=dst,
-            dst_ref=dst,
-            send_sem=send_sem.at[at],
-            recv_sem=recv_sem.at[at],
-            device_id=over(0, 0),
-            device_id_type=MESH,
-        )
-        when(flag, copy.wait_recv)
-
-    def send_rows(t):
-        remote(("hx", t, 0), nxt, hxpack.at[t, 0], hx.at[t, 0], same(1, 0))
-        remote(("hx", t, 1), prev, hxpack.at[t, 1], hx.at[t, 1], same(-1, 0))
-
-    def send_columns(t):
-        remote(("hz", t, 0), right, zpack.at[t], hz.at[t, 0], same(0, 1))
-        remote(("hz", t, 1), left, zpack.at[t], hz.at[t, 1], same(0, -1))
-
-    send_rows(0)
-    send_columns(0)
-    first, final_row = tiles.at[0, 0, 0], tiles.at[0, rows - 1, 0]
-    remote("es0", nxt, eff, eff_same.at[0], same(1, 0))
-    remote("es1", prev, eff, eff_same.at[1], same(-1, 0))
-    remote("eo0", nxt, eff, eff_over.at[0], over(1, 0))
-    remote("eo1", prev, eff, eff_over.at[1], over(-1, 0))
-    remote("wn0", nxt, wetm.at[rows - 8 : rows], wetn.at[0], same(1, 0))
-    remote("wn1", prev, wetm.at[0:8], wetn.at[1], same(-1, 0))
-    remote("wz0", right, wetm, wets.at[0], same(0, 1))
-    remote("wz1", left, wetm, wets.at[1], same(0, -1))
-
-    tile_copy.wait()
-    lane128 = lane_ids((128, 128))
-    packed = jnp.zeros((128, 128), BF16)
-    for k in range(depth):
-        for r in range(rows):
-            at = 2 * (k * rows + r)
-            packed = jnp.where(lane128 // 2 == at // 2, pltpu.roll(w[r, k], at + 1, 1), packed)
-    wcol[0:128] = packed
-    wcol[128:144] = jnp.concatenate([index, index], axis=0).astype(BF16)
-    for dx in (-1, 0, 1):
-        remote(("wc", 1 - dx), in_x[dx], wcol, wcols.at[1 - dx], over(dx, 0))
-    remote("we0", nxt, final_row, wedge.at[0], same(1, 0))
-    remote("we1", prev, first, wedge.at[1], same(-1, 0))
 
     def merged_edges(t):
         odd = lane_ids((24, 128)) % 2 == 1
@@ -423,6 +436,9 @@
                 send_parts(0, [mine[i] for i in range(rows)])
             column_inner(t + 1)
 
+        if final:
+            for flag, copy in sent[:-3]:
+                when(flag, copy.wait_send)
         receive(("ex", t, 1), None, box.at[rows : 2 * rows])
         receive(("ex", t, 0), prev, box.at[0:rows])
         receive(("ex", t, 2), nxt, box.at[2 * rows : 3 * rows])
@@ -430,8 +446,7 @@
             picks = [[], []]
             for i in range(2):
                 for k in range(depth):
-                    at = source_of(2 * p + i, k)
-                    picks[i].append(box[jnp.where(at >= 0, at, 3 * rows)])
+                    picks[i].append(box[chosen[depth * (2 * p + i) + k]])
             parts = pair_product(picks, (w[2 * p], w[2 * p + 1]))
             for i, r in enumerate((2 * p, 2 * p + 1)):
                 value = gains * wet[r : r + 1, :] * parts[i]
@@ -443,8 +458,9 @@
             if t == 0:
                 receive("es0", prev, eff_same.at[0])
                 receive("es1", nxt, eff_same.at[1])
-                receive("we0", prev, wedge.at[0])
-                receive("we1", nxt, wedge.at[1])
+                for part in parts_of_k:
+                    receive(("we", 0, part.start), prev, wedge.at[0, part])
+                    receive(("we", 1, part.start), nxt, wedge.at[1, part])
                 receive("wn0", prev, wetn.at[0])
                 receive("wn1", nxt, wetn.at[1])
                 receive("wz0", left, wets.at[0])
@@ -487,7 +503,7 @@
             )
             column_outer(t + 1)
 
-    for flag, copy in sent:
+    for flag, copy in sent[-3:]:
         when(flag, copy.wait_send)
 
 
@@ -547,6 +563,7 @@
             pltpu.SMEM((1, flux), F32),
             pltpu.SMEM((1, depth, 1, rows), jnp.int32),
             pltpu.SMEM((1, 1, rows), jnp.int32),
+            pltpu.SMEM((rows * depth,), jnp.int32),
             dma((24,)),
             dma((80,)),
             dma((80,)),

time: 37.6 us -> 37.5 us (level)
  no operation moved by 1% of the time
where the time goes in v5:
time: 37.5 us; the launch traced here: 37.4 us
  Pallas kernels  36.5 us (97%)
  local copies, waits for them, and re-layouts  0.92 us (2%)
    pallas_call x1, Pallas kernels, on_device(): pl.pallas_call(functools.partial(kernel, (lev, rows, flux, depth)), out_s...  36.5 us
    broadcast_in_dim x1, local copies, waits for them, and re-layouts, on_device(): return jnp.transpose(result, (1, 0, 2))[None]  0.92 us

profile of v5, /device:TPU:385, one launch (start us, length us, event | category | flops | bytes accessed | tf_op | source)
XLA Modules:
  0.0 37.4 jit_solution(13159144437334082226)
XLA Ops:
  0.0 36.5 %coupled.1 = f32[16,72,128]{2,1,0:T(8,128)S(1)} custom-call(f32[1,72,16,128]{3,2,1,0:T(8,128)} %fields.1, f32[1,16,128]{2,1,0:T(8,128)} %diff.1, s32[16,128]{1,0:T(8,128)} %wetm.1, f32[1,72,72]{2,1,0:T(8,128)} %op.1, f32[1,16]{1,0:T(1,128)} %scale_in.1, f32[1,16]{1,0:T(1,128)} %gain_in.1, s32[1,3,1,16]{3,2,1,0:T(1,128)} %bitcast.6, s32[1,1,16]{2,1,0:T(1,128)} %bitcast.7, ...), custom_call_target="tpu_custom_call" | custom-call | tf_op jit(solution)/shard_map/coupled/pallas_call | solution.py:519
  36.5 0.9 %copy.10 = f32[1,72,16,128]{3,2,1,0:T(8,128)} copy(f32[1,72,16,128]{3,1,2,0:T(8,128)S(1)} %bitcast.5) | data formatting | bytes 1179648 | tf_op jit(solution)/shard_map/broadcast_in_dim | solution.py:576

commit v6 on v4

--- a/solution.py
+++ b/solution.py
@@ -380,6 +380,11 @@
                 exported.append((jnp.tanh(scales * pair[i]) * wet[r : r + 1, :]).astype(BF16))
                 mine[r] = exported[r]
                 col[(*col_at(r), slice(0, flux))] = pair[i]
+            if p == pairs // 2 - 1:
+                half = rows // 2
+                for i, flag, dx in ((0, nxt, 1), (2, prev, -1)):
+                    at = i * rows
+                    remote(("eh", t, i, 0), flag, mine.at[0 * half : (0 + 1) * half], box.at[at + 0 * half : at + (0 + 1) * half], over(dx, 0))
         block = mine.at[0:rows]
 
         def send_exports():
@@ -387,7 +392,11 @@
             remote(("ex", t, 2), prev, block, box.at[2 * rows : 3 * rows], over(-1, 0))
             remote(("ex", t, 1), None, block, box.at[rows : 2 * rows], over(0, 0))
 
-        send_exports()
+        half = rows // 2
+        for i, flag, dx in ((0, nxt, 1), (2, prev, -1)):
+            at = i * rows
+            remote(("eh", t, i, 1), flag, mine.at[1 * half : (1 + 1) * half], box.at[at + 1 * half : at + (1 + 1) * half], over(dx, 0))
+        remote(("ex", t, 1), None, mine.at[0:rows], box.at[rows : 2 * rows], over(0, 0))
         if 0 < t < NSUB - 1:
             send_parts(t, exported)
         if not final:
@@ -424,8 +433,9 @@
             column_inner(t + 1)
 
         receive(("ex", t, 1), None, box.at[rows : 2 * rows])
-        receive(("ex", t, 0), prev, box.at[0:rows])
-        receive(("ex", t, 2), nxt, box.at[2 * rows : 3 * rows])
+        for h in range(2):
+            receive(("eh", t, 0, h), prev, box.at[h * half : (h + 1) * half])
+            receive(("eh", t, 2, h), nxt, box.at[2 * rows + h * half : 2 * rows + (h + 1) * half])
         for p in range(pairs):
             picks = [[], []]
             for i in range(2):

time: 37.6 us -> 37.6 us (level)
  no operation moved by 1% of the time
where the time goes in v6:
time: 37.6 us; the launch traced here: 37.4 us
  Pallas kernels  36.5 us (97%)
  local copies, waits for them, and re-layouts  0.92 us (2%)
    pallas_call x1, Pallas kernels, on_device(): pl.pallas_call(functools.partial(kernel, (lev, rows, flux, depth)), out_s...  36.5 us
    broadcast_in_dim x1, local copies, waits for them, and re-layouts, on_device(): return jnp.transpose(result, (1, 0, 2))[None]  0.92 us

profile of v6, /device:TPU:385, one launch (start us, length us, event | category | flops | bytes accessed | tf_op | source)
XLA Modules:
  0.0 37.4 jit_solution(15911277659641894753)
XLA Ops:
  0.0 36.5 %coupled.1 = f32[16,72,128]{2,1,0:T(8,128)S(1)} custom-call(f32[1,72,16,128]{3,2,1,0:T(8,128)} %fields.1, f32[1,16,128]{2,1,0:T(8,128)} %diff.1, s32[16,128]{1,0:T(8,128)} %wetm.1, f32[1,72,72]{2,1,0:T(8,128)} %op.1, f32[1,16]{1,0:T(1,128)} %scale_in.1, f32[1,16]{1,0:T(1,128)} %gain_in.1, s32[1,3,1,16]{3,2,1,0:T(1,128)} %bitcast.6, s32[1,1,16]{2,1,0:T(1,128)} %bitcast.7, ...), custom_call_target="tpu_custom_call" | custom-call | tf_op jit(solution)/shard_map/coupled/pallas_call | solution.py:513
  36.5 0.9 %copy.10 = f32[1,72,16,128]{3,2,1,0:T(8,128)} copy(f32[1,72,16,128]{3,1,2,0:T(8,128)S(1)} %bitcast.5) | data formatting | bytes 1179648 | tf_op jit(solution)/shard_map/broadcast_in_dim | solution.py:569
